TPU v7x, 256 devices: a whole 4x4x8 slice. The times are simulated.
256 devices in a mesh: row: 8 (over y, core), col: 32 (over x, z).
Axes of the slice: x: 4, y: 4, z: 8, core: 2. Of those that a mesh axis runs over, the one named last changes fastest.
Arguments:
- attn_grad: float32 [4, 4096, 4096], P(None, 'row', 'col'), may hold values from -54 to 54
- attn_param: float32 [4, 4096, 4096], P(None, 'row', 'col'), may hold values from -150 to 150
- attn_rows: float32 [4, 4096], P(None, 'row'), may hold values from 0.03 to 0.3
- attn_cols: float32 [4, 4096], P(None, 'col'), may hold values from 0.03 to 0.3
- wi_grad: float32 [2, 4096, 10240], P(None, 'row', 'col'), may hold values from -54 to 54
- wi_param: float32 [2, 4096, 10240], P(None, 'row', 'col'), may hold values from -150 to 150
- wi_rows: float32 [2, 4096], P(None, 'row'), may hold values from 4 to 40
- wi_cols: float32 [2, 10240], P(None, 'col'), may hold values from 4 to 40
- wo_grad: float32 [10240, 4096], P('row', 'col'), may hold values from -54 to 54
- wo_param: float32 [10240, 4096], P('row', 'col'), may hold values from -150 to 150
- wo_rows: float32 [10240], P('row'), may hold values from 4 to 40
- wo_cols: float32 [4096], P('col'), may hold values from 4 to 40
Outputs:
- attn_update: float32 [4, 4096, 4096], P(None, 'row', 'col')
- attn_rows_new: float32 [4, 4096], P(None, 'row')
- attn_cols_new: float32 [4, 4096], P(None, 'col')
- wi_update: float32 [2, 4096, 10240], P(None, 'row', 'col')
- wi_rows_new: float32 [2, 4096], P(None, 'row')
- wi_cols_new: float32 [2, 10240], P(None, 'col')
- wo_update: float32 [10240, 4096], P('row', 'col')
- wo_rows_new: float32 [10240], P('row')
- wo_cols_new: float32 [4096], P('col')
All inputs are finite; a program needn't handle non-finite values.
Results may differ from a plain program's by a relative error of at most 0.00002.
Values sent between devices are 32-bit elements; how exact they have to be, the bound alone decides.
No kernel may reach another device: no remote copies, remote signals or barrier semaphores. Data moves between devices by JAX's collectives and lax.ppermute only.
A program may use at most 64 MiB of HBM per device.

v0:
```python
import jax
import jax.numpy as jnp
from jax import lax
from jax.sharding import PartitionSpec as P

STEP = 2


EPS_SQUARE = 1e-30


def shards(
    attn_grad,
    attn_param,
    attn_rows,
    attn_cols,
    wi_grad,
    wi_param,
    wi_rows,
    wi_cols,
    wo_grad,
    wo_param,
    wo_rows,
    wo_cols,
):
    beta = 1.0 - STEP ** (-0.8)
    rho = STEP ** (-0.5)
    n_row = lax.axis_size("row")
    n_col = lax.axis_size("col")
    grads = (attn_grad, wi_grad, wo_grad[None])
    params = (attn_param, wi_param, wo_param[None])
    rows_old = (attn_rows, wi_rows, wo_rows[None])
    cols_old = (attn_cols, wi_cols, wo_cols[None])
    full_rows = tuple((g.shape[1] * n_row for g in grads))
    full_cols = tuple((g.shape[2] * n_col for g in grads))
    squares = tuple((g * g + EPS_SQUARE for g in grads))
    row_part = tuple((jnp.sum(s, axis=2) for s in squares))
    col_part = tuple((jnp.sum(s, axis=1) for s in squares))
    param_part = tuple((jnp.sum(p * p, axis=(1, 2)) for p in params))
    param_tot = lax.psum((param_part[0], param_part[1], param_part[2]), ("row", "col"))
    row_tot = lax.psum((row_part[0], row_part[1], row_part[2]), "col")
    col_tot = lax.psum((col_part[0], col_part[1], col_part[2]), "row")
    rows_new = tuple(
        (beta * rows_old[k] + (1.0 - beta) * (row_tot[k] / full_cols[k]) for k in range(3))
    )
    cols_new = tuple(
        (beta * cols_old[k] + (1.0 - beta) * (col_tot[k] / full_rows[k]) for k in range(3))
    )
    new_sum = tuple((jnp.sum(r, axis=1) for r in rows_new))
    level_tot = lax.psum((new_sum[0], new_sum[1], new_sum[2]), "row")
    levels = tuple((level_tot[k] / full_rows[k] for k in range(3)))
    directions = tuple(
        (
            grads[k]
            * lax.rsqrt(
                rows_new[k][:, :, None] * cols_new[k][:, None, :] / levels[k][:, None, None]
            )
            for k in range(3)
        )
    )
    dir_part = tuple((jnp.sum(d * d, axis=(1, 2)) for d in directions))
    dir_tot = lax.psum((dir_part[0], dir_part[1], dir_part[2]), ("row", "col"))
    updates = []
    for k in range(3):
        count = full_rows[k] * full_cols[k]
        dir_rms = jnp.sqrt(dir_tot[k] / count)
        param_rms = jnp.sqrt(param_tot[k] / count)
        factor = -rho * param_rms / jnp.maximum(1.0, dir_rms)
        updates.append(directions[k] * factor[:, None, None])
    return (
        updates[0],
        rows_new[0],
        cols_new[0],
        updates[1],
        rows_new[1],
        cols_new[1],
        updates[2][0],
        rows_new[2][0],
        cols_new[2][0],
    )


def solution(mesh):
    return jax.shard_map(
        shards,
        mesh=mesh,
        in_specs=(
            P(None, "row", "col"),
            P(None, "row", "col"),
            P(None, "row"),
            P(None, "col"),
            P(None, "row", "col"),
            P(None, "row", "col"),
            P(None, "row"),
            P(None, "col"),
            P("row", "col"),
            P("row", "col"),
            P("row"),
            P("col"),
        ),
        out_specs=(
            P(None, "row", "col"),
            P(None, "row"),
            P(None, "col"),
            P(None, "row", "col"),
            P(None, "row"),
            P(None, "col"),
            P("row", "col"),
            P("row"),
            P("col"),
        ),
        check_vma=False,
    )
```

profile of v0, /device:TPU:1, one launch (start us, length us, event | category | flops | bytes accessed | tf_op | source)
XLA Modules:
  0.0 247.8 jit_solution(16933708942639816038)
XLA Ops:
  0.6 0.0 copy-start.2
  0.7 0.0 copy-start.1
  0.7 0.0 copy-start.10
  0.7 2.0 multiply_reduce_fusion.5
  2.7 1.6 fusion
  4.3 0.0 copy-done.10
  4.3 0.0 copy-done.2
  4.3 0.3 fusion.4
  4.6 0.0 copy-done.1
  4.6 0.4 fusion.2
  5.0 118.7 %all-reduce.1 = (f32[4,512]{1,0:T(4,128)S(1)}, f32[2,512]{1,0:T(2,128)S(1)}, f32[1,1280]{1,0:T(1,128)S(1)}) all-reduce(f32[4,512]{1,0:T(4,128)S(1)} %get-tuple-element.12, f32[2,512]{1,0:T(2,128)S(1)} %get-tuple-element.10, f32[1,1280]{1,0:T(1,128)S(1)} %reduce_sum.156), channel_id=1, replica_groups=mesh['row'=8,'col'=32] {'col'}, use_global_device_ids=true, to_apply=%region_1.0 | all-reduce | flops 4352 | bytes 34816 | tf_op jit(solution)/shard_map/psum | solution.py:41
  123.7 0.0 copy-done.9
  123.7 0.1 fusion.9
  123.8 0.6 fusion.7
  124.4 0.0 copy-done.11
  124.4 0.1 fusion.8
  124.6 41.3 %all-reduce.2 = (f32[4]{0:T(128)S(1)}, f32[4,128]{1,0:T(4,128)S(1)}, f32[2]{0:T(128)S(1)}, f32[2,320]{1,0:T(2,128)S(1)}, f32[1]{0:T(128)}, /*index=5*/f32[1,128]{1,0:T(1,128)S(1)}) all-reduce(f32[4]{0:T(128)S(1)} %get-tuple-element.34, f32[4,128]{1,0:T(4,128)S(1)} %get-tuple-element.11, ...), channel_id=1, replica_groups=mesh['row'=8,'col'=32] {'row'}, use_global_device_ids=true, to_apply=%region_5.0 | all-reduce | flops 1287 | bytes 10296 | tf_op jit(solution)/shard_map/psum | solution.py:50
  166.6 0.0 copy-start.13
  166.6 0.0 copy-start.12
  166.6 0.0 copy-start
  166.6 0.0 copy-start.3
  166.6 0.8 multiply_reduce_fusion.4
  167.5 0.0 copy-done.14
  167.5 0.0 copy-start.8
  167.5 1.7 multiply_reduce_fusion.2
  169.3 0.0 copy-start.7
  169.3 0.6 multiply_reduce_fusion
  169.9 72.7 %all-reduce = (f32[4]{0:T(128)S(1)}, f32[4]{0:T(128)S(1)}, f32[2]{0:T(128)S(1)}, f32[2]{0:T(128)S(1)}, f32[1]{0:T(128)}, /*index=5*/f32[1]{0:T(128)}) all-reduce(f32[4]{0:T(128)S(1)} %get-tuple-element.38, f32[4]{0:T(128)S(1)} %get-tuple-element.39, f32[2]{0:T(128)S(1)} %get-tuple-element.36, ...), channel_id=1, replica_groups=mesh['row'=8,'col'=32] {'row','col'}, use_global_device_ids=true, to_apply=%region_9.0 | all-reduce | flops 14 | bytes 112 | tf_op jit(solution)/shard_map/psum | solution.py:62
  244.1 1.1 broadcast_multiply_fusion.2
  245.2 0.0 copy-done.4
  245.2 1.3 broadcast_multiply_fusion.1
  246.5 1.3 broadcast_multiply_fusion
  (25 shorter events, 0.1 us)
Async XLA Ops:
  0.6 3.7 %copy-start.2 = (f32[1280,128]{1,0:T(8,128)S(1)}, f32[1280,128]{1,0:T(8,128)}, u32[]{:S(2)}) copy-start(f32[1280,128]{1,0:T(8,128)} %param.20) | copy-start | bytes 1966084
  0.7 4.0 %copy-start.1 = (f32[4,512,128]{2,1,0:T(8,128)S(1)}, f32[4,512,128]{2,1,0:T(8,128)}, u32[]{:S(2)}) copy-start(f32[4,512,128]{2,1,0:T(8,128)} %param.12) | copy-start | bytes 3145732
  0.7 3.6 %copy-start.10 = (f32[1280]{0:T(1024)S(1)}, f32[1280]{0:T(1024)}, u32[]{:S(2)}) copy-start(f32[1280]{0:T(1024)} %param.22) | copy-start | bytes 15364
  2.7 121.0 %copy-start.9 = (f32[4,512]{1,0:T(4,128)S(1)}, f32[4,512]{1,0:T(4,128)}, u32[]{:S(2)}) copy-start(f32[4,512]{1,0:T(4,128)} %param.14) | copy-start | bytes 24580
  2.7 121.8 %copy-start.11 = (f32[2,512]{1,0:T(2,128)S(1)}, f32[2,512]{1,0:T(2,128)}, u32[]{:S(2)}) copy-start(f32[2,512]{1,0:T(2,128)} %param.18) | copy-start | bytes 12292
  2.7 163.9 %copy-start.15 = (f32[128]{0:T(128)S(1)}, f32[128]{0:T(128)}, u32[]{:S(2)}) copy-start(f32[128]{0:T(128)} %param.23) | copy-start | bytes 1540
  4.3 163.2 %copy-start.14 = (f32[4,128]{1,0:T(4,128)S(1)}, f32[4,128]{1,0:T(4,128)}, u32[]{:S(2)}) copy-start(f32[4,128]{1,0:T(4,128)} %param.15) | copy-start | bytes 6148
  123.8 121.3 %copy-start.4 = (f32[4,512]{1,0:T(4,128)}, f32[4,512]{1,0:T(4,128)S(1)}, u32[]{:S(2)}) copy-start(f32[4,512]{1,0:T(4,128)S(1)} %get-tuple-element.35) | copy-start | bytes 24580
  124.4 119.6 %copy-start.5 = (f32[1280]{0:T(1024)}, f32[1280]{0:T(1024)S(1)}, u32[]{:S(2)}) copy-start(f32[1280]{0:T(1024)S(1)} %get-tuple-element.15) | copy-start | bytes 15364
  124.6 121.9 %copy-start.6 = (f32[2,512]{1,0:T(2,128)}, f32[2,512]{1,0:T(2,128)S(1)}, u32[]{:S(2)}) copy-start(f32[2,512]{1,0:T(2,128)S(1)} %get-tuple-element.33) | copy-start | bytes 12292
  166.6 77.5 %copy-start.13 = (f32[128]{0:T(128)}, f32[128]{0:T(128)S(1)}, u32[]{:S(2)}) copy-start(f32[128]{0:T(128)S(1)} %fusion.6) | copy-start | bytes 1540
  166.6 2.6 %copy-start.12 = (f32[2,320]{1,0:T(2,128)S(1)}, f32[2,320]{1,0:T(2,128)}, u32[]{:S(2)}) copy-start(f32[2,320]{1,0:T(2,128)} %param.19) | copy-start | bytes 7684
  166.6 2.6 %copy-start = (f32[2,512,320]{1,2,0:T(8,128)S(1)}, f32[2,512,320]{1,2,0:T(8,128)}, u32[]{:S(2)}) copy-start(f32[2,512,320]{1,2,0:T(8,128)} %param.16) | copy-start | bytes 3932164
  166.6 2.6 %copy-start.3 = (f32[2,512,320]{1,2,0:T(8,128)S(1)}, f32[2,512,320]{1,2,0:T(8,128)}, u32[]{:S(2)}) copy-start(f32[2,512,320]{1,2,0:T(8,128)} %param.17) | copy-start | bytes 3932164
  167.5 77.7 %copy-start.8 = (f32[4,128]{1,0:T(4,128)}, f32[4,128]{1,0:T(4,128)S(1)}, u32[]{:S(2)}) copy-start(f32[4,128]{1,0:T(4,128)S(1)} %multiply_add_fusion.7) | copy-start | bytes 6148
  169.3 77.2 %copy-start.7 = (f32[2,320]{1,0:T(2,128)}, f32[2,320]{1,0:T(2,128)S(1)}, u32[]{:S(2)}) copy-start(f32[2,320]{1,0:T(2,128)S(1)} %multiply_add_fusion.6) | copy-start | bytes 7684
where the time goes:
time: 248 us
  blocking collectives  233 us (94%)
  other arithmetic  12.1 us (5%)
  between operations  2.93 us (1%)
    psum x1, blocking collectives, shards(): row_tot = lax.psum((row_part[0], row_part[1], row_part[2]), 'col')  119 us
    psum x1, blocking collectives, shards(): dir_tot = lax.psum((dir_part[0], dir_part[1], dir_part[2]), ('row', 'col'))  72.7 us
    psum x1, blocking collectives, shards(): level_tot = lax.psum((new_sum[0], new_sum[1], new_sum[2]), 'row')  41.3 us

commit v1 on v0

v1 whole, which is shorter than its diff:
```python
import jax
import jax.numpy as jnp
from jax import lax
from jax.sharding import Mesh, PartitionSpec as P

STEP = 2
EPS_SQUARE = 1e-30
LANES = 128
ROW = ("y", "core")
COL = ("x", "z")


def one_shot_sum(x, axes, n):
    sent = jnp.broadcast_to(x[None], (n,) + x.shape)
    return jnp.sum(lax.all_to_all(sent, axes, 0, 0), axis=0)


def pack(parts):
    flat = jnp.concatenate([p.reshape(-1) for p in parts])
    pad = -flat.shape[0] % LANES
    return jnp.pad(flat, (0, pad)).reshape(-1, LANES)


def unpack(packed, shapes):
    flat = packed.reshape(-1)
    out, at = [], 0
    for s in shapes:
        size = 1
        for d in s:
            size *= d
        out.append(flat[at : at + size].reshape(s))
        at += size
    return out


def shards(
    attn_grad,
    attn_param,
    attn_rows,
    attn_cols,
    wi_grad,
    wi_param,
    wi_rows,
    wi_cols,
    wo_grad,
    wo_param,
    wo_rows,
    wo_cols,
):
    beta = 1.0 - STEP ** (-0.8)
    rho = STEP ** (-0.5)
    n_row = lax.axis_size(ROW)
    n_x = lax.axis_size("x")
    n_z = lax.axis_size("z")
    grads = (attn_grad, wi_grad, wo_grad[None])
    params = (attn_param, wi_param, wo_param[None])
    rows_old = (attn_rows, wi_rows, wo_rows[None])
    cols_old = (attn_cols, wi_cols, wo_cols[None])
    full_rows = tuple(g.shape[1] * n_row for g in grads)
    full_cols = tuple(g.shape[2] * n_x * n_z for g in grads)
    col_part = [jnp.sum(g * g + EPS_SQUARE, axis=1) for g in grads]
    col_tot = unpack(one_shot_sum(pack(col_part), ROW, n_row), [c.shape for c in col_part])
    cols_new = [beta * cols_old[k] + (1.0 - beta) * (col_tot[k] / full_rows[k]) for k in range(3)]
    row_part = [jnp.sum(g * g + EPS_SQUARE, axis=2) for g in grads]
    inv_cols = [1.0 / c for c in cols_new]
    scaled = [jnp.sum(g * g * v[:, None, :], axis=2) for g, v in zip(grads, inv_cols)]
    param_part = [jnp.sum(p * p, axis=(1, 2)) for p in params]
    parts = row_part + scaled + param_part
    shapes = [p.shape for p in parts]
    tot = one_shot_sum(pack(parts), "x", n_x)
    tot = unpack(one_shot_sum(tot, "z", n_z), shapes)
    row_tot, scaled_tot, param_col = tot[0:3], tot[3:6], tot[6:9]
    rows_new = [beta * rows_old[k] + (1.0 - beta) * (row_tot[k] / full_cols[k]) for k in range(3)]
    new_sum = [jnp.sum(r, axis=1) for r in rows_new]
    ratio = [jnp.sum(s / r, axis=1) for s, r in zip(scaled_tot, rows_new)]
    scalars = new_sum + ratio + param_col
    shapes = [s.shape for s in scalars]
    tot = unpack(one_shot_sum(pack(scalars), ROW, n_row), shapes)
    updates = []
    for k in range(3):
        count = full_rows[k] * full_cols[k]
        level = tot[k] / full_rows[k]
        dir_rms = jnp.sqrt(level * tot[3 + k] / count)
        param_rms = jnp.sqrt(tot[6 + k] / count)
        factor = -rho * param_rms / jnp.maximum(1.0, dir_rms) * jnp.sqrt(level)
        left = lax.rsqrt(rows_new[k]) * factor[:, None]
        right = lax.rsqrt(cols_new[k])
        updates.append(grads[k] * (left[:, :, None] * right[:, None, :]))
    return (
        updates[0],
        rows_new[0],
        cols_new[0],
        updates[1],
        rows_new[1],
        cols_new[1],
        updates[2][0],
        rows_new[2][0],
        cols_new[2][0],
    )


def solution(mesh):
    fine = Mesh(mesh.devices.reshape(4, 2, 4, 8), ("y", "core", "x", "z"))
    return jax.shard_map(
        shards,
        mesh=fine,
        in_specs=(
            P(None, ROW, COL),
            P(None, ROW, COL),
            P(None, ROW),
            P(None, COL),
            P(None, ROW, COL),
            P(None, ROW, COL),
            P(None, ROW),
            P(None, COL),
            P(ROW, COL),
            P(ROW, COL),
            P(ROW),
            P(COL),
        ),
        out_specs=(
            P(None, ROW, COL),
            P(None, ROW),
            P(None, COL),
            P(None, ROW, COL),
            P(None, ROW),
            P(None, COL),
            P(ROW, COL),
            P(ROW),
            P(COL),
        ),
        check_vma=False,
    )
```

time: 248 us -> 65.8 us (0.27)
  blocking collectives: 233 us -> 25.9 us
  starting transfers between devices: 0 us -> 13.6 us
  waiting for transfers between devices: 0 us -> 5.68 us
  local copies, waits for them, and re-layouts: 0.08 us -> 4.29 us
    psum x3 -> x0, blocking collectives: 233 us -> none  [the longest x1 119 us: shards(): row_tot = lax.psum((row_part[0], row_part[1], row_part[2]), 'col')]
    all_to_all x0 -> x2, blocking collectives: none -> 25.9 us  [one_shot_sum(): return jnp.sum(lax.all_to_all(sent, axes, 0, 0), axis=0)]
    all_to_all x0 -> x2, starting transfers between devices: none -> 13.6 us  [one_shot_sum(): return jnp.sum(lax.all_to_all(sent, axes, 0, 0), axis=0)]
    all_to_all x0 -> x2, waiting for transfers between devices: none -> 5.68 us  [one_shot_sum(): return jnp.sum(lax.all_to_all(sent, axes, 0, 0), axis=0)]
    reduce_sum x9 -> x16, other arithmetic: 7.66 us -> 8.86 us  [the longest x3 3.66 us: shards(): param_part = [jnp.sum(p * p, axis=(1, 2)) for p in params]]
  transfers between devices with their start and end apart: 0 -> 2, of which waited for: 0 -> 2; matrix products, arithmetic and copies ran while one was open for 0% -> 6% of each run, Pallas kernels for 0% -> 0%
where the time goes in v1:
time: 65.8 us; the launch traced here: 65.4 us
  blocking collectives  25.9 us (39%)
  starting transfers between devices  13.6 us (21%)
  other arithmetic  12.9 us (20%)
  waiting for transfers between devices  5.68 us (9%)
  local copies, waits for them, and re-layouts  4.29 us (7%)
  between operations  3.07 us (5%)
    all_to_all x2, blocking collectives, one_shot_sum(): return jnp.sum(lax.all_to_all(sent, axes, 0, 0), axis=0)  25.9 us
    all_to_all x2, starting transfers between devices, one_shot_sum(): return jnp.sum(lax.all_to_all(sent, axes, 0, 0), axis=0)  13.6 us
    all_to_all x2, waiting for transfers between devices, one_shot_sum(): return jnp.sum(lax.all_to_all(sent, axes, 0, 0), axis=0)  5.68 us
    reduce_sum x3, other arithmetic, shards(): param_part = [jnp.sum(p * p, axis=(1, 2)) for p in params]  3.66 us
    mul x3, other arithmetic, shards(): updates.append(grads[k] * (left[:, :, None] * right[:, None, :]))  3.63 us
    reduce_sum x3, other arithmetic, shards(): col_part = [jnp.sum(g * g + EPS_SQUARE, axis=1) for g in grads]  2.93 us
    concatenate x2, local copies, waits for them, and re-layouts, pack(): flat = jnp.concatenate([p.reshape(-1) for p in parts])  2.11 us
  transfers between devices with their start and end apart: 2, of which 2 were waited for; matrix products, arithmetic and copies ran while one was open for 6% of the time, Pallas kernels for 0%

profile of v1, /device:TPU:1, one launch (start us, length us, event | category | flops | bytes accessed | tf_op | source)
XLA Modules:
  0.0 65.4 jit_solution(2602941941385312524)
XLA Ops:
  0.7 1.4 %add_reduce_fusion.4 = f32[128]{0:T(128)S(1)} fusion(f32[1280,128]{1,0:T(8,128)} %param.20), kind=kLoop, calls=%fused_computation.13 | loop fusion | flops 491392 | bytes 655872 | tf_op jit(solution)/shard_map/reduce_sum | solution.py:61
  2.0 1.3 %add_reduce_fusion.2 = f32[4,128]{1,0:T(4,128)S(1)} fusion(f32[4,512,128]{2,1,0:T(8,128)} %param.12), kind=kLoop, calls=%fused_computation.8 | loop fusion | flops 785920 | bytes 1050624 | tf_op jit(solution)/shard_map/reduce_sum | solution.py:61
  3.4 0.2 add_reduce_fusion
  3.6 0.1 reshape.241
  3.7 0.6 broadcast_in_dim.13
  4.3 6.5 %all-to-all-start = ((f32[8,10,128]{2,1,0:T(8,128)}), f32[8,10,128]{2,1,0:T(8,128)S(1)}, u32[]{:S(2)}, u32[]{:S(2)}) async-start(f32[8,10,128]{2,1,0:T(8,128)} %broadcast_in_dim.13), calls=%async_computation | async-start | bytes 131072 | tf_op jit(solution)/shard_map/all_to_all | solution.py:15
  10.8 1.4 %multiply_reduce_fusion.2 = f32[4]{0:T(128)S(1)} fusion(f32[4,512,128]{2,1,0:T(8,128)} %param.13), kind=kLoop, calls=%fused_computation.6 | loop fusion | flops 524284 | bytes 1048592 | tf_op jit(solution)/shard_map/reduce_sum | solution.py:67
  12.3 0.3 multiply_reduce_fusion
  12.6 1.9 %multiply_reduce_fusion.4 = f32[]{:T(128)} fusion(f32[1280,128]{1,0:T(8,128)} %param.21), kind=kLoop, calls=%fused_computation.11 | loop fusion | flops 327679 | bytes 655364 | tf_op jit(solution)/shard_map/reduce_sum | solution.py:67
  14.5 1.2 %all-to-all-done = f32[8,10,128]{2,1,0:T(8,128)S(1)} async-done(((f32[8,10,128]{2,1,0:T(8,128)}), f32[8,10,128]{2,1,0:T(8,128)S(1)}, u32[]{:S(2)}, u32[]{:S(2)}) %all-to-all-start) | async-done | bytes 40992 | tf_op jit(solution)/shard_map/all_to_all | solution.py:15
  15.8 0.1 mul.297
  15.9 0.2 multiply_reduce_fusion.1
  16.2 0.6 multiply_reduce_fusion.3
  16.9 0.4 multiply_reduce_fusion.5
  17.3 0.7 %concatenate.11 = f32[8711]{0:T(1024)S(1)} concatenate(f32[2048]{0:T(1024)S(1)} %bitcast.47, f32[1024]{0:T(1024)S(1)} %bitcast.51, f32[1280]{0:T(1024)S(1)} %get-tuple-element.14, f32[2048]{0:T(1024)S(1)} %bitcast.46, f32[1024]{0:T(1024)S(1)} %bitcast.50, f32[1280]{0:T(1024)S(1)} %get-tuple-element.13, f32[4]{0:T(128)S(1)} %multiply_reduce_fusion.2, f32[2]{0:T(128)S(1)} %multiply_reduce_fusion, ...), dimensions={0} | concatenate | bytes 69688 | tf_op jit(solution)/shard_map/concatenate | solution.py:19
  18.1 8.2 %all_to_all.20 = f32[4,69,128]{2,1,0:T(8,128)S(1)} all-to-all(f32[4,69,128]{2,1,0:T(8,128)S(1)} %broadcast_in_dim.15), channel_id=1, replica_groups=mesh['y'=4,'core'=2,'x'=4,'z'=8] {'x'}, dimensions={0} | all-to-all | bytes 282624 | tf_op jit(solution)/shard_map/all_to_all | solution.py:15
  26.3 17.7 %all_to_all.21 = f32[8,69,128]{2,1,0:T(8,128)S(1)} all-to-all(f32[8,69,128]{2,1,0:T(8,128)S(1)} %broadcast_in_dim.16), channel_id=1, replica_groups=mesh['y'=4,'core'=2,'x'=4,'z'=8] {'z'}, dimensions={0} | all-to-all | bytes 565248 | tf_op jit(solution)/shard_map/all_to_all | solution.py:15
  44.1 0.6 fusion.3
  44.7 0.2 divide_reduce_fusion.1
  44.9 0.2 divide_reduce_fusion
  45.1 1.4 %concatenate.12 = f32[21]{0:T(128)S(1)} concatenate(f32[4]{0:T(128)S(1)} %get-tuple-element.18, f32[2]{0:T(128)S(1)} %get-tuple-element.20, f32[1]{0:T(128)} %bitcast.6, f32[4]{0:T(128)S(1)} %get-tuple-element.17, f32[2]{0:T(128)S(1)} %get-tuple-element.19, f32[1]{0:T(128)} %bitcast.8, f32[7]{0:T(128)S(1)} %slice.106), dimensions={0} | concatenate | bytes 168 | tf_op jit(solution)/shard_map/concatenate | solution.py:19
  46.5 0.6 broadcast_in_dim.17
  47.1 7.1 %all-to-all-start.3 = ((f32[8,1,128]{2,1,0:T(1,128)}), f32[8,1,128]{2,1,0:T(1,128)S(1)}, u32[]{:S(2)}, u32[]{:S(2)}) async-start(f32[8,1,128]{2,1,0:T(1,128)} %broadcast_in_dim.17), calls=%async_computation.3 | async-start | bytes 8192 | tf_op jit(solution)/shard_map/all_to_all | solution.py:15
  54.2 4.5 %all-to-all-done.3 = f32[8,1,128]{2,1,0:T(1,128)S(1)} async-done(((f32[8,1,128]{2,1,0:T(1,128)}), f32[8,1,128]{2,1,0:T(1,128)S(1)}, u32[]{:S(2)}, u32[]{:S(2)}) %all-to-all-start.3) | async-done | bytes 4128 | tf_op jit(solution)/shard_map/all_to_all | solution.py:15
  58.7 0.1 multiply_bitcast_fusion.1
  58.8 0.1 multiply_bitcast_fusion
  58.9 0.6 fusion.12
  61.6 0.1 rsqrt_multiply_fusion.2
  61.7 0.1 rsqrt_multiply_fusion.1
  61.7 1.1 %multiply_multiply_fusion.2 = f32[1280,128]{1,0:T(8,128)} fusion(f32[1280,128]{1,0:T(8,128)S(1)} %copy-done.2, f32[128]{0:T(128)S(1)} %get-tuple-element.21, f32[1280]{0:T(1024)S(1)} %rsqrt_multiply_fusion), kind=kLoop, calls=%fused_computation.10 | loop fusion | flops 327680 | bytes 1316352 | tf_op jit(solution)/shard_map/mul | solution.py:88
  62.8 1.3 %multiply_multiply_fusion.1 = f32[4,512,128]{2,1,0:T(8,128)} fusion(f32[4,512,128]{2,1,0:T(8,128)S(1)} %copy-done.1, f32[4,128]{1,0:T(4,128)S(1)} %rsqrt.21, f32[4,512]{1,0:T(4,128)S(1)} %rsqrt_multiply_fusion.1), kind=kLoop, calls=%fused_computation.5 | loop fusion | flops 524288 | bytes 2107392 | tf_op jit(solution)/shard_map/mul | solution.py:88
  64.1 1.2 %multiply_multiply_fusion = f32[2,512,320]{1,2,0:T(8,128)} fusion(f32[2,512,320]{1,2,0:T(8,128)S(1)} %copy-done, f32[2,320]{1,0:T(2,128)S(1)} %get-tuple-element.23, f32[2,512]{1,0:T(2,128)S(1)} %rsqrt_multiply_fusion.2), kind=kLoop, calls=%fused_computation | loop fusion | flops 655360 | bytes 2628096 | tf_op jit(solution)/shard_map/mul | solution.py:88
  (60 shorter events, 0.3 us)
Async XLA Ops:
  0.6 2.7 %copy-start = (f32[2,512,320]{1,2,0:T(8,128)S(1)}, f32[2,512,320]{1,2,0:T(8,128)}, u32[]{:S(2)}) copy-start(f32[2,512,320]{1,2,0:T(8,128)} %param.16) | copy-start | bytes 3932164
  3.4 8.9 %copy-start.3 = (f32[2,512,320]{1,2,0:T(8,128)S(1)}, f32[2,512,320]{1,2,0:T(8,128)}, u32[]{:S(2)}) copy-start(f32[2,512,320]{1,2,0:T(8,128)} %param.17) | copy-start | bytes 3932164
  4.3 11.4 %all-to-all-start = ((f32[8,10,128]{2,1,0:T(8,128)}), f32[8,10,128]{2,1,0:T(8,128)S(1)}, u32[]{:S(2)}, u32[]{:S(2)}) async-start(f32[8,10,128]{2,1,0:T(8,128)} %broadcast_in_dim.13), calls=%async_computation | async-start | bytes 131072 | tf_op jit(solution)/shard_map/all_to_all | solution.py:15
  10.8 4.9 %copy-start.14 = (f32[128]{0:T(128)S(1)}, f32[128]{0:T(128)}, u32[]{:S(2)}) copy-start(f32[128]{0:T(128)} %param.23) | copy-start | bytes 1540
  10.8 4.9 %copy-start.13 = (f32[4,128]{1,0:T(4,128)S(1)}, f32[4,128]{1,0:T(4,128)}, u32[]{:S(2)}) copy-start(f32[4,128]{1,0:T(4,128)} %param.15) | copy-start | bytes 6148
  10.8 5.1 %copy-start.12 = (f32[2,320]{1,0:T(2,128)S(1)}, f32[2,320]{1,0:T(2,128)}, u32[]{:S(2)}) copy-start(f32[2,320]{1,0:T(2,128)} %param.19) | copy-start | bytes 7684
  12.6 3.6 %copy-start.1 = (f32[4,512,128]{2,1,0:T(8,128)S(1)}, f32[4,512,128]{2,1,0:T(8,128)}, u32[]{:S(2)}) copy-start(f32[4,512,128]{2,1,0:T(8,128)} %param.12) | copy-start | bytes 3145732
  14.5 2.3 %copy-start.2 = (f32[1280,128]{1,0:T(8,128)S(1)}, f32[1280,128]{1,0:T(8,128)}, u32[]{:S(2)}) copy-start(f32[1280,128]{1,0:T(8,128)} %param.20) | copy-start | bytes 1966084
  15.7 1.6 %copy-start.15 = (f32[128]{0:T(128)}, f32[128]{0:T(128)S(1)}, u32[]{:S(2)}) copy-start(f32[128]{0:T(128)S(1)} %get-tuple-element.22) | copy-start | bytes 1540
  15.8 38.4 %copy-start.8 = (f32[4,128]{1,0:T(4,128)}, f32[4,128]{1,0:T(4,128)S(1)}, u32[]{:S(2)}) copy-start(f32[4,128]{1,0:T(4,128)S(1)} %get-tuple-element.29) | copy-start | bytes 6148
  15.9 1.4 %copy-start.7 = (f32[2,320]{1,0:T(2,128)}, f32[2,320]{1,0:T(2,128)S(1)}, u32[]{:S(2)}) copy-start(f32[2,320]{1,0:T(2,128)S(1)} %get-tuple-element.24) | copy-start | bytes 7684
  16.9 27.2 %copy-start.9 = (f32[1280]{0:T(1024)S(1)}, f32[1280]{0:T(1024)}, u32[]{:S(2)}) copy-start(f32[1280]{0:T(1024)} %param.22) | copy-start | bytes 15364
  16.9 27.9 %copy-start.11 = (f32[2,512]{1,0:T(2,128)S(1)}, f32[2,512]{1,0:T(2,128)}, u32[]{:S(2)}) copy-start(f32[2,512]{1,0:T(2,128)} %param.18) | copy-start | bytes 12292
  16.9 28.0 %copy-start.10 = (f32[4,512]{1,0:T(4,128)S(1)}, f32[4,512]{1,0:T(4,128)}, u32[]{:S(2)}) copy-start(f32[4,512]{1,0:T(4,128)} %param.14) | copy-start | bytes 24580
  44.7 19.4 %copy-start.4 = (f32[1280]{0:T(1024)}, f32[1280]{0:T(1024)S(1)}, u32[]{:S(2)}) copy-start(f32[1280]{0:T(1024)S(1)} %get-tuple-element.25) | copy-start | bytes 15364
  44.9 19.2 %copy-start.6 = (f32[2,512]{1,0:T(2,128)}, f32[2,512]{1,0:T(2,128)S(1)}, u32[]{:S(2)}) copy-start(f32[2,512]{1,0:T(2,128)S(1)} %get-tuple-element.26) | copy-start | bytes 12292
  45.1 19.1 %copy-start.5 = (f32[4,512]{1,0:T(4,128)}, f32[4,512]{1,0:T(4,128)S(1)}, u32[]{:S(2)}) copy-start(f32[4,512]{1,0:T(4,128)S(1)} %get-tuple-element.27) | copy-start | bytes 24580
  47.1 11.6 %all-to-all-start.3 = ((f32[8,1,128]{2,1,0:T(1,128)}), f32[8,1,128]{2,1,0:T(1,128)S(1)}, u32[]{:S(2)}, u32[]{:S(2)}) async-start(f32[8,1,128]{2,1,0:T(1,128)} %broadcast_in_dim.17), calls=%async_computation.3 | async-start | bytes 8192 | tf_op jit(solution)/shard_map/all_to_all | solution.py:15

commit v2 on v0

v2 whole, which is shorter than its diff:
```python
import jax
import jax.numpy as jnp
from jax import lax
from jax.experimental import pallas as pl
from jax.experimental.pallas import tpu as pltpu
from jax.sharding import Mesh, PartitionSpec as P

STEP = 2
EPS_SQUARE = 1e-30
BETA = 1.0 - STEP ** (-0.8)
RHO = STEP ** (-0.5)
LANES = 128
N_MATS = 7

ROW = ("y", "core")
COL = ("x", "zq", "zp")
NEAR = ("x", "zp")
FAR = ("zq",)

A_MATS, A_ROWS = 4, 512
W_MATS, W_COLS, W_ROWS = 2, 320, 512
O_ROWS = 1280
A_TILES, O_TILES, W_TILES = A_ROWS // LANES, O_ROWS // LANES, W_ROWS // LANES
W_COL_TILES = -(-W_COLS // LANES)

C_WI, C_WO, C_ALL = 4, 10, 16
R_WI, R_WO, R_ALL = 16, 24, 34
S_PARAM, S_ALL = 2 * R_ALL, 72

VMEM_LIMIT = 48 * 1024 * 1024
WHOLE = pl.BlockSpec(memory_space=pltpu.VMEM)
ANYWHERE = pl.BlockSpec(memory_space=pl.ANY)


def call(body, out_shape, in_specs, out_specs, scratch=(), bytes_accessed=1 << 20, aliases=None):
    return pl.pallas_call(
        body,
        out_shape=out_shape,
        in_specs=in_specs,
        out_specs=out_specs,
        scratch_shapes=list(scratch),
        input_output_aliases=aliases or {},
        compiler_params=pltpu.CompilerParams(vmem_limit_bytes=VMEM_LIMIT),
        cost_estimate=pl.CostEstimate(flops=4 << 20, bytes_accessed=bytes_accessed, transcendentals=0),
    )


def here(x):
    return pltpu.with_memory_space_constraint(x, pltpu.VMEM)


def far(x):
    return pltpu.with_memory_space_constraint(x, pltpu.HBM)


def f32(*shape):
    return jax.ShapeDtypeStruct(shape, jnp.float32)


def vmem(*shape):
    return pltpu.VMEM(shape, jnp.float32)


def hbm(*shape):
    return pltpu.HBM(shape, jnp.float32)


def grad_copies(sources, targets, sems):
    a, w, o = sources
    a_to, w_to, o_to = targets
    pairs = [(a.at[k], a_to.at[k]) for k in range(A_MATS)]
    pairs += [(w.at[k], w_to.at[k]) for k in range(W_MATS)]
    pairs += [(o, o_to)]
    return [pltpu.make_async_copy(s, t, sems.at[i]) for i, (s, t) in enumerate(pairs)]


def total(x):
    return jnp.sum(x, axis=0, keepdims=True)


def as_column(row):
    return jnp.broadcast_to(row, (LANES, LANES)).T


def load_kernel(a, w, o, send, ga, gw, go, packed, sems):
    copies = grad_copies((a, w, o), (ga, gw, go), sems)
    for c in copies:
        c.start()
    packed[...] = jnp.zeros_like(packed)
    for k in range(A_MATS):
        copies[k].wait()
        g = ga[k]
        packed[k : k + 1, :] = total(g * g + EPS_SQUARE)
    for k in range(W_MATS):
        copies[A_MATS + k].wait()
        for b in range(W_COL_TILES):
            lo, hi = b * LANES, min((b + 1) * LANES, W_COLS)
            folded = jnp.zeros((hi - lo, LANES), jnp.float32)
            for t in range(W_TILES):
                g = gw[k, lo:hi, t * LANES : (t + 1) * LANES]
                folded = folded + (g * g + EPS_SQUARE)
            if hi - lo < LANES:
                folded = jnp.concatenate([folded, jnp.zeros((LANES - hi + lo, LANES), jnp.float32)], axis=0)
            at = C_WI + k * W_COL_TILES + b
            packed[at : at + 1, :] = total(folded.T)
    copies[-1].wait()
    g = go[...]
    packed[C_WO : C_WO + 1, :] = total(g * g + EPS_SQUARE)
    value = packed[...]
    for n in range(send.shape[0]):
        send[n] = value


def wi_places():
    for k in range(W_MATS):
        for b in range(W_COL_TILES):
            lo, hi = b * LANES, min((b + 1) * LANES, W_COLS)
            yield k, C_WI + k * W_COL_TILES + b, lo, hi


def row_places():
    for k in range(A_MATS):
        for t in range(A_TILES):
            yield 0, k, t, k * A_TILES + t
    for k in range(W_MATS):
        for t in range(W_TILES):
            yield 1, k, t, R_WI + k * W_TILES + t


def rows_kernel(ga, gw, go, pa, pw, po, ar, wr, orr, ac, wc, oc, ta, to, packed, old_rows, old_cols, qa, qw, qo, sums, sems):
    copies = grad_copies((pa, pw, po), (qa, qw, qo), sems)
    for c in copies:
        c.start()
    old_rows[...] = jnp.zeros_like(old_rows)
    for which, k, t, at in row_places():
        old_rows[at : at + 1, :] = (ar, wr)[which][k : k + 1, t * LANES : (t + 1) * LANES]
    old_rows[R_WO:R_ALL, :] = orr[...]
    old_cols[...] = jnp.ones_like(old_cols)
    old_cols[0:A_MATS, :] = ac[...]
    for k, at, lo, hi in wi_places():
        old_cols[at : at + 1, 0 : hi - lo] = wc[k : k + 1, lo:hi]
    old_cols[C_WO : C_WO + 1, :] = oc[...]
    for k in range(A_MATS):
        for t in range(A_TILES):
            tile = slice(t * LANES, (t + 1) * LANES)
            g = ga[k, tile, :].T
            ta[k, tile, :] = g
            at = k * A_TILES + t
            packed[at : at + 1, :] = total(g * g + EPS_SQUARE)
    for t in range(O_TILES):
        tile = slice(t * LANES, (t + 1) * LANES)
        g = go[tile, :].T
        to[tile, :] = g
        packed[R_WO + t : R_WO + t + 1, :] = total(g * g + EPS_SQUARE)
    for k in range(W_MATS):
        for t in range(W_TILES):
            g = gw[k, :, t * LANES : (t + 1) * LANES]
            at = R_WI + k * W_TILES + t
            packed[at : at + 1, :] = total(g * g + EPS_SQUARE)
    sums[...] = jnp.zeros_like(sums)
    for k in range(A_MATS):
        copies[k].wait()
        p = qa[k]
        sums[k : k + 1, :] = total(p * p)
    for k in range(W_MATS):
        copies[A_MATS + k].wait()
        folded = jnp.zeros((W_COLS, LANES), jnp.float32)
        for t in range(W_TILES):
            p = qw[k, :, t * LANES : (t + 1) * LANES]
            folded = folded + p * p
        sums[A_MATS + k : A_MATS + k + 1, :] = total(folded)
    copies[-1].wait()
    p = qo[...]
    sums[N_MATS - 1 : N_MATS, :] = total(p * p)
    each = jnp.sum(sums[...], axis=1, keepdims=True)
    sub = lax.broadcasted_iota(jnp.int32, (8, LANES), 0)
    lane = lax.broadcasted_iota(jnp.int32, (8, LANES), 1)
    packed[R_ALL : R_ALL + 1, :] = total(jnp.where(sub == lane, each, 0.0))
    packed[R_ALL + 1 :, :] = jnp.zeros((packed.shape[0] - R_ALL - 1, LANES), jnp.float32)


def cols_kernel(got, old_cols, row_sums, ta, gw, to, send, cols, packed):
    tot = got[0]
    for n in range(1, got.shape[0]):
        tot = tot + got[n]
    at = lax.broadcasted_iota(jnp.int32, (C_ALL, LANES), 0)
    full_a, full_o = float(A_ROWS * got.shape[0]), float(O_ROWS * got.shape[0])
    mean = tot / jnp.where(at == C_WO, full_o, full_a)
    new = BETA * old_cols[...] + (1.0 - BETA) * mean
    cols[...] = new
    inv = 1.0 / new
    packed[0:R_ALL, :] = row_sums[0:R_ALL, :]
    packed[S_PARAM:S_ALL, :] = row_sums[R_ALL : R_ALL + S_ALL - S_PARAM, :]
    for k in range(A_MATS):
        weight = as_column(inv[k : k + 1, :])
        for t in range(A_TILES):
            at = R_ALL + k * A_TILES + t
            g = ta[k, t * LANES : (t + 1) * LANES, :]
            packed[at : at + 1, :] = total(g * g * weight)
    weight = as_column(inv[C_WO : C_WO + 1, :])
    for t in range(O_TILES):
        at = R_ALL + R_WO + t
        g = to[t * LANES : (t + 1) * LANES, :]
        packed[at : at + 1, :] = total(g * g * weight)
    for k in range(W_MATS):
        sums = [jnp.zeros((8, LANES), jnp.float32) for _ in range(W_TILES)]
        for b in range(W_COL_TILES):
            lo, hi = b * LANES, min((b + 1) * LANES, W_COLS)
            at = C_WI + k * W_COL_TILES + b
            weight = as_column(inv[at : at + 1, :])[0 : hi - lo, :]
            for t in range(W_TILES):
                g = gw[k, lo:hi, t * LANES : (t + 1) * LANES]
                part = (g * g * weight).reshape((hi - lo) // 8, 8, LANES)
                sums[t] = sums[t] + jnp.sum(part, axis=0)
        for t in range(W_TILES):
            at = R_ALL + R_WI + k * W_TILES + t
            packed[at : at + 1, :] = total(sums[t])
    value = packed[...]
    for n in range(send.shape[0]):
        send[n] = value


def relay_kernel(got, send):
    tot = got[0]
    for n in range(1, got.shape[0]):
        tot = tot + got[n]
    for n in range(send.shape[0]):
        send[n] = tot


def new_rows_kernel(n_col, got, old_rows, send, rows, tot, ratio):
    value = got[0]
    for n in range(1, got.shape[0]):
        value = value + got[n]
    tot[...] = value
    at = lax.broadcasted_iota(jnp.int32, (R_ALL, LANES), 0)
    full_a, full_w = float(LANES * n_col), float(W_COLS * n_col)
    full = jnp.where((at >= R_WI) & (at < R_WO), full_w, full_a)
    new = BETA * old_rows[0:R_ALL, :] + (1.0 - BETA) * (tot[0:R_ALL, :] / full)
    rows[0:R_ALL, :] = new
    rows[R_ALL:, :] = jnp.ones((rows.shape[0] - R_ALL, LANES), jnp.float32)
    ratio[...] = tot[R_ALL : 2 * R_ALL, :] / new
    spans = [(k * A_TILES, (k + 1) * A_TILES) for k in range(A_MATS)]
    spans += [(R_WI + k * W_TILES, R_WI + (k + 1) * W_TILES) for k in range(W_MATS)]
    spans += [(R_WO, R_ALL)]
    sub = lax.broadcasted_iota(jnp.int32, (8, LANES), 0)
    lane = lax.broadcasted_iota(jnp.int32, (8, LANES), 1)
    levels = jnp.zeros((8, LANES), jnp.float32)
    ratios = jnp.zeros((8, LANES), jnp.float32)
    for k, (lo, hi) in enumerate(spans):
        levels = jnp.where(sub == k, total(rows[lo:hi, :]), levels)
        ratios = jnp.where(sub == k, total(ratio[lo:hi, :]), ratios)
    params = jnp.where(sub == lane, tot[S_PARAM : S_PARAM + 1, :], 0.0)
    levels = jnp.sum(levels, axis=1, keepdims=True)
    ratios = jnp.sum(ratios, axis=1, keepdims=True)
    params = jnp.sum(params, axis=1, keepdims=True)
    value = jnp.where(lane < 32, levels, jnp.where(lane < 64, ratios, params))
    for n in range(send.shape[0]):
        send[n] = value


def scaled_kernel(ta, gw, to, rows, cols, ua, uw, uo, ar, wr, orr, ac, wc, oc):
    for which, k, t, at in row_places():
        (ar, wr)[which][k : k + 1, t * LANES : (t + 1) * LANES] = rows[at : at + 1, :]
    orr[...] = rows[R_WO:R_ALL, :]
    ac[...] = cols[0:A_MATS, :]
    for k, at, lo, hi in wi_places():
        wc[k : k + 1, lo:hi] = cols[at : at + 1, 0 : hi - lo]
    oc[...] = cols[C_WO : C_WO + 1, :]
    left = lax.rsqrt(rows[0:R_ALL, :])
    right = lax.rsqrt(cols[...])
    for k in range(A_MATS):
        column = as_column(right[k : k + 1, :])
        for t in range(A_TILES):
            at = k * A_TILES + t
            tile = slice(t * LANES, (t + 1) * LANES)
            ua[k, tile, :] = (ta[k, tile, :] * column * left[at : at + 1, :]).T
    column = as_column(right[C_WO : C_WO + 1, :])
    for t in range(O_TILES):
        at = R_WO + t
        tile = slice(t * LANES, (t + 1) * LANES)
        uo[tile, :] = (to[tile, :] * column * left[at : at + 1, :]).T
    for k, at, lo, hi in wi_places():
        column = as_column(right[at : at + 1, :])[0 : hi - lo, :]
        for t in range(W_TILES):
            row = R_WI + k * W_TILES + t
            tile = slice(t * LANES, (t + 1) * LANES)
            uw[k, lo:hi, tile] = gw[k, lo:hi, tile] * column * left[row : row + 1, :]


def update_kernel(n_col, got, ua, uw, uo, a, w, o, va, vw, vo, sems):
    tot = got[0]
    for n in range(1, got.shape[0]):
        tot = tot + got[n]
    sub = lax.broadcasted_iota(jnp.int32, (8, 1), 0)
    n_row = got.shape[0]
    full_rows = jnp.where(sub == N_MATS - 1, float(O_ROWS * n_row), float(A_ROWS * n_row))
    wide = (sub >= A_MATS) & (sub < A_MATS + W_MATS)
    full_cols = jnp.where(wide, float(W_COLS * n_col), float(LANES * n_col))
    count = full_rows * full_cols
    level = tot[:, 0:1] / full_rows
    dir_rms = jnp.sqrt(level * tot[:, 32:33] / count)
    param_rms = jnp.sqrt(tot[:, 64:65] / count)
    factor = -RHO * param_rms / jnp.maximum(1.0, dir_rms) * jnp.sqrt(level)
    copies = grad_copies((va, vw, vo), (a, w, o), sems)
    for k in range(A_MATS):
        va[k] = ua[k] * factor[k : k + 1, :]
        copies[k].start()
    for k in range(W_MATS):
        vw[k] = uw[k] * factor[A_MATS + k : A_MATS + k + 1, :]
        copies[A_MATS + k].start()
    vo[...] = uo[...] * factor[N_MATS - 1 : N_MATS, :]
    copies[-1].start()
    for c in copies:
        c.wait()


def exchange(x, axes):
    return lax.all_to_all(x, axes, 0, 0)


def shards(
    attn_grad,
    attn_param,
    attn_rows,
    attn_cols,
    wi_grad,
    wi_param,
    wi_rows,
    wi_cols,
    wo_grad,
    wo_param,
    wo_rows,
    wo_cols,
):
    n_row, n_near, n_far = (lax.axis_size(axes) for axes in (ROW, NEAR, FAR))
    n_col = n_near * n_far
    wi_grad = jnp.swapaxes(wi_grad, 1, 2)
    wi_param = jnp.swapaxes(wi_param, 1, 2)
    blocks = ((A_MATS, A_ROWS, LANES), (W_MATS, W_COLS, W_ROWS), (O_ROWS, LANES))
    held = [vmem(*b) for b in blocks]
    sems = pltpu.SemaphoreType.DMA((N_MATS,))
    send, ga, gw, go = call(
        load_kernel,
        [f32(n_row, C_ALL, LANES)] + held,
        [ANYWHERE] * 3,
        [WHOLE] * 4,
        [vmem(C_ALL, LANES), sems],
        bytes_accessed=3 << 20,
    )(far(attn_grad), far(wi_grad), far(wo_grad))
    got = exchange(send, ROW)
    ga, gw, go = here(ga), here(gw), here(go)
    ta, to, row_sums, old_rows, old_cols = call(
        rows_kernel,
        [held[0], held[2], vmem(40, LANES), vmem(40, LANES), vmem(C_ALL, LANES)],
        [WHOLE] * 3 + [ANYWHERE] * 3 + [WHOLE] * 6,
        [WHOLE] * 5,
        held + [vmem(8, LANES), sems],
        bytes_accessed=6 << 20,
        aliases={0: 0, 2: 1},
    )(
        ga,
        gw,
        go,
        far(attn_param),
        far(wi_param),
        far(wo_param),
        attn_rows,
        wi_rows,
        wo_rows.reshape(O_TILES, LANES),
        attn_cols,
        wi_cols,
        wo_cols.reshape(1, LANES),
    )
    ta, to = here(ta), here(to)
    send, cols = call(
        cols_kernel,
        [f32(n_near, S_ALL, LANES), vmem(C_ALL, LANES)],
        [WHOLE] * 6,
        [WHOLE] * 2,
        [vmem(S_ALL, LANES)],
        bytes_accessed=3 << 20,
    )(got, here(old_cols), here(row_sums), ta, gw, to)
    got = exchange(send, NEAR)
    send = call(relay_kernel, f32(n_far, S_ALL, LANES), [WHOLE], WHOLE)(got)
    got = exchange(send, FAR)
    send, rows = call(
        lambda *refs: new_rows_kernel(n_col, *refs),
        [f32(n_row, 8, LANES), vmem(40, LANES)],
        [WHOLE] * 2,
        [WHOLE] * 2,
        [vmem(S_ALL, LANES), vmem(R_ALL, LANES)],
    )(got, here(old_rows))
    got = exchange(send, ROW)
    ua, uw, uo, attn_rows_new, wi_rows_new, wo_rows_new, attn_cols_new, wi_cols_new, wo_cols_new = call(
        scaled_kernel,
        held
        + [
            f32(A_MATS, A_ROWS),
            f32(W_MATS, W_ROWS),
            f32(O_TILES, LANES),
            f32(A_MATS, LANES),
            f32(W_MATS, W_COLS),
            f32(1, LANES),
        ],
        [WHOLE] * 5,
        [WHOLE] * 9,
        bytes_accessed=6 << 20,
        aliases={0: 0, 1: 1, 2: 2},
    )(ta, gw, to, here(rows), here(cols))
    attn_update, wi_update, wo_update = call(
        lambda *refs: update_kernel(n_col, *refs),
        [hbm(*b) for b in blocks],
        [WHOLE] * 4,
        [ANYWHERE] * 3,
        held + [sems],
        bytes_accessed=3 << 20,
    )(got, here(ua), here(uw), here(uo))
    return (
        attn_update,
        attn_rows_new,
        attn_cols_new,
        jnp.swapaxes(wi_update, 1, 2),
        wi_rows_new,
        wi_cols_new,
        wo_update,
        wo_rows_new.reshape(O_ROWS),
        wo_cols_new.reshape(LANES),
    )


def solution(mesh):
    fine = Mesh(mesh.devices.reshape(4, 2, 4, 4, 2), ROW + COL)
    big, row, col = P(None, ROW, COL), P(None, ROW), P(None, COL)
    return jax.shard_map(
        shards,
        mesh=fine,
        in_specs=(big, big, row, col, big, big, row, col, P(ROW, COL), P(ROW, COL), P(ROW), P(COL)),
        out_specs=(big, row, col, big, row, col, P(ROW, COL), P(ROW), P(COL)),
        check_vma=False,
    )
```

time: 248 us -> 55.5 us (0.22)
  blocking collectives: 233 us -> 25.6 us
  starting transfers between devices: 0 us -> 13.4 us
  other arithmetic: 12.1 us -> 0 us
  Pallas kernels: 0 us -> 10.3 us
  waiting for transfers between devices: 0 us -> 5.11 us
    psum x3 -> x0, blocking collectives: 233 us -> none  [the longest x1 119 us: shards(): row_tot = lax.psum((row_part[0], row_part[1], row_part[2]), 'col')]
    all_to_all x0 -> x2, blocking collectives: none -> 25.6 us  [exchange(): return lax.all_to_all(x, axes, 0, 0)]
    all_to_all x0 -> x2, starting transfers between devices: none -> 13.4 us  [exchange(): return lax.all_to_all(x, axes, 0, 0)]
    pallas_call x0 -> x7, Pallas kernels: none -> 10.3 us  [the longest x1 2.81 us: shards(): call(rows_kernel, [held[0], held[2], vmem(40, LANES), vmem(40, LANES), vm...]
    reduce_sum x9 -> x0, other arithmetic: 7.66 us -> none  [the longest x3 3.18 us: shards(): dir_part = tuple((jnp.sum(d * d, axis=(1, 2)) for d in directions))]
    all_to_all x0 -> x2, waiting for transfers between devices: none -> 5.11 us  [exchange(): return lax.all_to_all(x, axes, 0, 0)]
    mul x5 -> x0, other arithmetic: 3.77 us -> none  [the longest x3 3.76 us: shards(): updates.append(directions[k] * factor[:, None, None])]
  transfers between devices with their start and end apart: 0 -> 2, of which waited for: 0 -> 2; matrix products, arithmetic and copies ran while one was open for 0% -> 0% of each run, Pallas kernels for 0% -> 8%
where the time goes in v2:
time: 55.5 us; the launch traced here: 55.1 us
  blocking collectives  25.6 us (46%)
  starting transfers between devices  13.4 us (24%)
  Pallas kernels  10.3 us (19%)
  waiting for transfers between devices  5.11 us (9%)
  between operations  0.75 us (1%)
    all_to_all x2, blocking collectives, exchange(): return lax.all_to_all(x, axes, 0, 0)  25.6 us
    all_to_all x2, starting transfers between devices, exchange(): return lax.all_to_all(x, axes, 0, 0)  13.4 us
    all_to_all x2, waiting for transfers between devices, exchange(): return lax.all_to_all(x, axes, 0, 0)  5.11 us
    pallas_call x1, Pallas kernels, shards(): call(rows_kernel, [held[0], held[2], vmem(40, LANES), vmem(40, LANES), vm...  2.81 us
    pallas_call x1, Pallas kernels, shards(): call(load_kernel, [f32(n_row, C_ALL, LANES)] + held, [ANYWHERE] * 3, [WHO...  2.7 us
    pallas_call x1, Pallas kernels, shards(): call(lambda *refs: update_kernel(n_col, *refs), [hbm(*b) for b in blocks]...  1.95 us
    pallas_call x1, Pallas kernels, shards(): call(scaled_kernel, held + [f32(A_MATS, A_ROWS), f32(W_MATS, W_ROWS), f32...  1.63 us
  transfers between devices with their start and end apart: 2, of which 2 were waited for; matrix products, arithmetic and copies ran while one was open for 0% of the time, Pallas kernels for 8%

profile of v2, /device:TPU:1, one launch (start us, length us, event | category | flops | bytes accessed | tf_op | source)
XLA Modules:
  0.0 55.1 jit_solution(15055364386559761527)
XLA Ops:
  0.6 0.0 copy-start
  0.7 0.0 copy-start.1
  0.7 0.0 copy-start.2
  0.7 0.0 copy-start.3
  0.7 0.0 copy-start.4
  0.7 0.0 copy-start.5
  0.7 2.7 %shard_map.187 = (f32[8,16,128]{2,1,0:T(8,128)}, f32[4,512,128]{2,1,0:T(8,128)S(1)}, f32[2,320,512]{2,1,0:T(8,128)S(1)}, f32[1280,128]{1,0:T(8,128)S(1)}) custom-call(f32[4,512,128]{2,1,0:T(8,128)} %a.1, f32[2,320,512]{2,1,0:T(8,128)} %bitcast.9, f32[1280,128]{1,0:T(8,128)} %o.1), custom_call_target="tpu_custom_call" | custom-call | flops 4194304 | bytes 3145728 | tf_op jit(solution)/shard_map/pallas_call | solution.py:343
  3.4 6.5 %all-to-all-start = ((f32[8,16,128]{2,1,0:T(8,128)}), f32[8,16,128]{2,1,0:T(8,128)S(1)}, u32[]{:S(2)}, u32[]{:S(2)}) async-start(f32[8,16,128]{2,1,0:T(8,128)} %get-tuple-element.34), calls=%async_computation | async-start | bytes 131072 | tf_op jit(solution)/shard_map/all_to_all | solution.py:319
  9.9 0.0 copy-done
  9.9 0.0 copy-done.1
  9.9 0.0 copy-done.2
  9.9 0.0 copy-done.3
  10.0 0.0 copy-done.4
  10.0 0.0 copy-done.5
  10.0 2.8 %shard_map.188 = (f32[4,512,128]{2,1,0:T(8,128)S(1)}, f32[1280,128]{1,0:T(8,128)S(1)}, f32[40,128]{1,0:T(8,128)S(1)}, f32[40,128]{1,0:T(8,128)S(1)}, f32[16,128]{1,0:T(8,128)S(1)}) custom-call(f32[4,512,128]{2,1,0:T(8,128)S(1)} %get-tuple-element.35.ga, f32[2,320,512]{2,1,0:T(8,128)S(1)} %get-tuple-element.36.gw, ...), custom_call_target="tpu_custom_call", output_to_operand_aliasing={{0}: (0, {}), {1}: (2, {})} | custom-call | flops 4194304 | bytes 6291456 | tf_op jit(solution)/shard_map/pallas_call | solution.py:353
  12.8 2.0 %all-to-all-done.got = f32[8,16,128]{2,1,0:T(8,128)S(1)} async-done(((f32[8,16,128]{2,1,0:T(8,128)}), f32[8,16,128]{2,1,0:T(8,128)S(1)}, u32[]{:S(2)}, u32[]{:S(2)}) %all-to-all-start) | async-done | bytes 65568 | tf_op jit(solution)/shard_map/all_to_all | solution.py:319
  14.8 0.4 shard_map.189
  15.2 11.2 %all_to_all.20.got = f32[8,72,128]{2,1,0:T(8,128)S(1)} all-to-all(f32[8,72,128]{2,1,0:T(8,128)S(1)} %get-tuple-element.42), channel_id=1, replica_groups=mesh['y'=4,'core'=2,'x'=4,'zq'=4,'zp'=2] {'x','zp'}, dimensions={0} | all-to-all | bytes 589824 | tf_op jit(solution)/shard_map/all_to_all | solution.py:319
  26.4 14.4 %all_to_all.21.refs_0_ = f32[4,72,128]{2,1,0:T(8,128)S(1)} all-to-all(f32[4,72,128]{2,1,0:T(8,128)S(1)} %shard_map.190), channel_id=1, replica_groups=mesh['y'=4,'core'=2,'x'=4,'zq'=4,'zp'=2] {'zq'}, dimensions={0} | all-to-all | bytes 294912 | tf_op jit(solution)/shard_map/all_to_all | solution.py:319
  40.8 0.7 %shard_map.191 = (f32[8,8,128]{2,1,0:T(8,128)}, f32[40,128]{1,0:T(8,128)S(1)}) custom-call(f32[4,72,128]{2,1,0:T(8,128)S(1)} %all_to_all.21.refs_0_, f32[40,128]{1,0:T(8,128)S(1)} %get-tuple-element.43.refs_1_), custom_call_target="tpu_custom_call" | custom-call | flops 4194304 | bytes 1048576 | tf_op jit(solution)/shard_map/pallas_call | solution.py:387
  41.5 6.9 %all-to-all-start.3 = ((f32[8,8,128]{2,1,0:T(8,128)}), f32[8,8,128]{2,1,0:T(8,128)S(1)}, u32[]{:S(2)}, u32[]{:S(2)}) async-start(f32[8,8,128]{2,1,0:T(8,128)} %get-tuple-element.44), calls=%async_computation.3 | async-start | bytes 65536 | tf_op jit(solution)/shard_map/all_to_all | solution.py:319
  48.5 1.6 %shard_map.192 = (f32[4,512,128]{2,1,0:T(8,128)S(1)}, f32[2,320,512]{2,1,0:T(8,128)S(1)}, f32[1280,128]{1,0:T(8,128)S(1)}, f32[4,512]{1,0:T(4,128)}, f32[2,512]{...) custom-call(f32[4,512,128]{2,1,0:T(8,128)S(1)} %get-tuple-element.40, ...), custom_call_target="tpu_custom_call", output_to_operand_aliasing={{0}: (0, {}), {1}: (1, {}), {2}: (2, {})} | custom-call | flops 4194304 | bytes 6291456 | tf_op jit(solution)/shard_map/pallas_call | solution.py:395
  50.1 3.1 %all-to-all-done.3.refs_0_ = f32[8,8,128]{2,1,0:T(8,128)S(1)} async-done(((f32[8,8,128]{2,1,0:T(8,128)}), f32[8,8,128]{2,1,0:T(8,128)S(1)}, u32[]{:S(2)}, u32[]{:S(2)}) %all-to-all-start.3) | async-done | bytes 32800 | tf_op jit(solution)/shard_map/all_to_all | solution.py:319
  53.2 2.0 %shard_map.193 = (f32[4,512,128]{2,1,0:T(8,128)}, f32[2,320,512]{2,1,0:T(8,128)}, f32[1280,128]{1,0:T(8,128)}) custom-call(f32[8,8,128]{2,1,0:T(8,128)S(1)} %all-to-all-done.3.refs_0_, f32[4,512,128]{2,1,0:T(8,128)S(1)} %get-tuple-element.47.refs_1_, f32[2,320,512]{2,1,0:T(8,128)S(1)} %get-tuple-element.48.refs_2_, f32[1280,128]{1,0:T(8,128)S(1)} %get-tuple-element.49.refs_3_), custom_call_target="tpu_custom_call" | custom-call | flops 4194304 | bytes 3145728 | tf_op jit(solution)/shard_map/pallas_call | solution.py:411
  (1 shorter events, 0.0 us)
Async XLA Ops:
  0.6 9.3 %copy-start = (f32[4,512]{1,0:T(4,128)S(1)}, f32[4,512]{1,0:T(4,128)}, u32[]{:S(2)}) copy-start(f32[4,512]{1,0:T(4,128)} %ar.1) | copy-start | bytes 24580
  0.7 9.3 %copy-start.1 = (f32[1280]{0:T(1024)S(1)}, f32[1280]{0:T(1024)}, u32[]{:S(2)}) copy-start(f32[1280]{0:T(1024)} %param.22) | copy-start | bytes 15364
  0.7 9.3 %copy-start.2 = (f32[2,512]{1,0:T(2,128)S(1)}, f32[2,512]{1,0:T(2,128)}, u32[]{:S(2)}) copy-start(f32[2,512]{1,0:T(2,128)} %wr.1) | copy-start | bytes 12292
  0.7 9.3 %copy-start.3 = (f32[2,320]{1,0:T(2,128)S(1)}, f32[2,320]{1,0:T(2,128)}, u32[]{:S(2)}) copy-start(f32[2,320]{1,0:T(2,128)} %wc.1) | copy-start | bytes 7684
  0.7 9.3 %copy-start.4 = (f32[4,128]{1,0:T(4,128)S(1)}, f32[4,128]{1,0:T(4,128)}, u32[]{:S(2)}) copy-start(f32[4,128]{1,0:T(4,128)} %ac.1) | copy-start | bytes 6148
  0.7 9.3 %copy-start.5 = (f32[128]{0:T(128)S(1)}, f32[128]{0:T(128)}, u32[]{:S(2)}) copy-start(f32[128]{0:T(128)} %param.23) | copy-start | bytes 1540
  3.4 11.4 %all-to-all-start = ((f32[8,16,128]{2,1,0:T(8,128)}), f32[8,16,128]{2,1,0:T(8,128)S(1)}, u32[]{:S(2)}, u32[]{:S(2)}) async-start(f32[8,16,128]{2,1,0:T(8,128)} %get-tuple-element.34), calls=%async_computation | async-start | bytes 131072 | tf_op jit(solution)/shard_map/all_to_all | solution.py:319
  41.5 11.7 %all-to-all-start.3 = ((f32[8,8,128]{2,1,0:T(8,128)}), f32[8,8,128]{2,1,0:T(8,128)S(1)}, u32[]{:S(2)}, u32[]{:S(2)}) async-start(f32[8,8,128]{2,1,0:T(8,128)} %get-tuple-element.44), calls=%async_computation.3 | async-start | bytes 65536 | tf_op jit(solution)/shard_map/all_to_all | solution.py:319

commit v3 on v2

--- a/solution.py
+++ b/solution.py
@@ -26,6 +26,8 @@
 C_WI, C_WO, C_ALL = 4, 10, 16
 R_WI, R_WO, R_ALL = 16, 24, 34
 S_PARAM, S_ALL = 2 * R_ALL, 72
+
+N_WRITES = 3 + 2 * W_MATS + (A_MATS * A_TILES + O_TILES) // 2
 
 VMEM_LIMIT = 48 * 1024 * 1024
 WHOLE = pl.BlockSpec(memory_space=pltpu.VMEM)
@@ -224,15 +226,11 @@
     tot = got[0]
     for n in range(1, got.shape[0]):
         tot = tot + got[n]
-    for n in range(send.shape[0]):
-        send[n] = tot
-
-
-def new_rows_kernel(n_col, got, old_rows, send, rows, tot, ratio):
-    value = got[0]
-    for n in range(1, got.shape[0]):
-        value = value + got[n]
-    tot[...] = value
+    send[...] = tot
+
+
+def new_rows_kernel(n_col, old_rows, done, own, before, after, opposite, send, rows, tot, ratio):
+    tot[...] = (own[...] + opposite[...]) + (before[...] + after[...])
     at = lax.broadcasted_iota(jnp.int32, (R_ALL, LANES), 0)
     full_a, full_w = float(LANES * n_col), float(W_COLS * n_col)
     full = jnp.where((at >= R_WI) & (at < R_WO), full_w, full_a)
@@ -259,36 +257,42 @@
         send[n] = value
 
 
-def scaled_kernel(ta, gw, to, rows, cols, ua, uw, uo, ar, wr, orr, ac, wc, oc):
-    for which, k, t, at in row_places():
-        (ar, wr)[which][k : k + 1, t * LANES : (t + 1) * LANES] = rows[at : at + 1, :]
-    orr[...] = rows[R_WO:R_ALL, :]
+def scaled_kernel(ta, gw, to, cols, after, ua, uw, uo, ac, wc, oc, done):
+    done[...] = jnp.zeros_like(done)
     ac[...] = cols[0:A_MATS, :]
     for k, at, lo, hi in wi_places():
         wc[k : k + 1, lo:hi] = cols[at : at + 1, 0 : hi - lo]
     oc[...] = cols[C_WO : C_WO + 1, :]
-    left = lax.rsqrt(rows[0:R_ALL, :])
     right = lax.rsqrt(cols[...])
     for k in range(A_MATS):
         column = as_column(right[k : k + 1, :])
         for t in range(A_TILES):
-            at = k * A_TILES + t
             tile = slice(t * LANES, (t + 1) * LANES)
-            ua[k, tile, :] = (ta[k, tile, :] * column * left[at : at + 1, :]).T
+            ua[k, tile, :] = ta[k, tile, :] * column
     column = as_column(right[C_WO : C_WO + 1, :])
     for t in range(O_TILES):
-        at = R_WO + t
         tile = slice(t * LANES, (t + 1) * LANES)
-        uo[tile, :] = (to[tile, :] * column * left[at : at + 1, :]).T
+        uo[tile, :] = to[tile, :] * column
     for k, at, lo, hi in wi_places():
         column = as_column(right[at : at + 1, :])[0 : hi - lo, :]
         for t in range(W_TILES):
-            row = R_WI + k * W_TILES + t
             tile = slice(t * LANES, (t + 1) * LANES)
-            uw[k, lo:hi, tile] = gw[k, lo:hi, tile] * column * left[row : row + 1, :]
-
-
-def update_kernel(n_col, got, ua, uw, uo, a, w, o, va, vw, vo, sems):
+            uw[k, lo:hi, tile] = gw[k, lo:hi, tile] * column
+
+
+def update_kernel(n_col, got, rows, ua, uw, uo, a, w, o, ar, wr, orr, va, vw, vo, var, vwr, sems):
+    small = [(var, ar), (vwr, wr), (rows.at[R_WO:R_ALL, :], orr)]
+    copies = [pltpu.make_async_copy(s, t, sems.at[i]) for i, (s, t) in enumerate(small)]
+    for which, k, t, at in row_places():
+        (var, vwr)[which][k : k + 1, t * LANES : (t + 1) * LANES] = rows[at : at + 1, :]
+    for c in copies:
+        c.start()
+
+    def write(source, target):
+        copies.append(pltpu.make_async_copy(source, target, sems.at[len(copies)]))
+        copies[-1].start()
+
+    left = lax.rsqrt(rows[0:R_ALL, :])
     tot = got[0]
     for n in range(1, got.shape[0]):
         tot = tot + got[n]
@@ -302,21 +306,44 @@
     dir_rms = jnp.sqrt(level * tot[:, 32:33] / count)
     param_rms = jnp.sqrt(tot[:, 64:65] / count)
     factor = -RHO * param_rms / jnp.maximum(1.0, dir_rms) * jnp.sqrt(level)
-    copies = grad_copies((va, vw, vo), (a, w, o), sems)
-    for k in range(A_MATS):
-        va[k] = ua[k] * factor[k : k + 1, :]
-        copies[k].start()
-    for k in range(W_MATS):
-        vw[k] = uw[k] * factor[A_MATS + k : A_MATS + k + 1, :]
-        copies[A_MATS + k].start()
-    vo[...] = uo[...] * factor[N_MATS - 1 : N_MATS, :]
-    copies[-1].start()
+    for k in range(W_MATS):
+        f = factor[A_MATS + k : A_MATS + k + 1, :]
+        scale = [left[R_WI + k * W_TILES + t : R_WI + k * W_TILES + t + 1, :] * f for t in range(W_TILES)]
+        for lo, hi in ((0, W_COLS // 2), (W_COLS // 2, W_COLS)):
+            for t in range(W_TILES):
+                tile = slice(t * LANES, (t + 1) * LANES)
+                vw[k, lo:hi, tile] = uw[k, lo:hi, tile] * scale[t]
+            write(vw.at[k, lo:hi], w.at[k, lo:hi])
+    for k in range(A_MATS):
+        f = factor[k : k + 1, :]
+        for t in range(A_TILES):
+            at = k * A_TILES + t
+            tile = slice(t * LANES, (t + 1) * LANES)
+            va[k, tile, :] = (ua[k, tile, :] * (left[at : at + 1, :] * f)).T
+            if t % 2:
+                half = slice((t - 1) * LANES, (t + 1) * LANES)
+                write(va.at[k, half], a.at[k, half])
+    f = factor[N_MATS - 1 : N_MATS, :]
+    for t in range(O_TILES):
+        at = R_WO + t
+        tile = slice(t * LANES, (t + 1) * LANES)
+        vo[tile, :] = (uo[tile, :] * (left[at : at + 1, :] * f)).T
+        if t % 2:
+            half = slice((t - 1) * LANES, (t + 1) * LANES)
+            write(vo.at[half], o.at[half])
     for c in copies:
         c.wait()
 
 
 def exchange(x, axes):
     return lax.all_to_all(x, axes, 0, 0)
+
+
+def quad(x, axis, order):
+    got = {0: x}
+    for shift in order:
+        got[shift] = lax.ppermute(x, axis, [(i, (i + shift) % 4) for i in range(4)])
+    return [got[shift] for shift in (0, 1, 3, 2)]
 
 
 def shards(
@@ -382,40 +409,32 @@
         bytes_accessed=3 << 20,
     )(got, here(old_cols), here(row_sums), ta, gw, to)
     got = exchange(send, NEAR)
-    send = call(relay_kernel, f32(n_far, S_ALL, LANES), [WHOLE], WHOLE)(got)
-    got = exchange(send, FAR)
+    send = call(relay_kernel, f32(S_ALL, LANES), [WHOLE], WHOLE)(got)
+    got = quad(send, "zq", (1, 3, 2))
+    ua, uw, uo, attn_cols_new, wi_cols_new, wo_cols_new, done = call(
+        scaled_kernel,
+        held + [f32(A_MATS, LANES), f32(W_MATS, W_COLS), f32(1, LANES), vmem(8, LANES)],
+        [WHOLE] * 4 + [ANYWHERE],
+        [WHOLE] * 7,
+        bytes_accessed=6 << 20,
+        aliases={0: 0, 1: 1, 2: 2},
+    )(ta, gw, to, here(cols), send)
     send, rows = call(
         lambda *refs: new_rows_kernel(n_col, *refs),
         [f32(n_row, 8, LANES), vmem(40, LANES)],
-        [WHOLE] * 2,
+        [WHOLE, ANYWHERE] + [WHOLE] * 4,
         [WHOLE] * 2,
         [vmem(S_ALL, LANES), vmem(R_ALL, LANES)],
-    )(got, here(old_rows))
+    )(here(old_rows), here(done), *got)
     got = exchange(send, ROW)
-    ua, uw, uo, attn_rows_new, wi_rows_new, wo_rows_new, attn_cols_new, wi_cols_new, wo_cols_new = call(
-        scaled_kernel,
-        held
-        + [
-            f32(A_MATS, A_ROWS),
-            f32(W_MATS, W_ROWS),
-            f32(O_TILES, LANES),
-            f32(A_MATS, LANES),
-            f32(W_MATS, W_COLS),
-            f32(1, LANES),
-        ],
+    attn_update, wi_update, wo_update, attn_rows_new, wi_rows_new, wo_rows_new = call(
+        lambda *refs: update_kernel(n_col, *refs),
+        [hbm(*b) for b in blocks] + [hbm(A_MATS, A_ROWS), hbm(W_MATS, W_ROWS), hbm(O_TILES, LANES)],
         [WHOLE] * 5,
-        [WHOLE] * 9,
-        bytes_accessed=6 << 20,
-        aliases={0: 0, 1: 1, 2: 2},
-    )(ta, gw, to, here(rows), here(cols))
-    attn_update, wi_update, wo_update = call(
-        lambda *refs: update_kernel(n_col, *refs),
-        [hbm(*b) for b in blocks],
-        [WHOLE] * 4,
-        [ANYWHERE] * 3,
-        held + [sems],
+        [ANYWHERE] * 6,
+        held + [vmem(A_MATS, A_ROWS), vmem(W_MATS, W_ROWS), pltpu.SemaphoreType.DMA((N_WRITES,))],
         bytes_accessed=3 << 20,
-    )(got, here(ua), here(uw), here(uo))
+    )(got, here(rows), here(ua), here(uw), here(uo))
     return (
         attn_update,
         attn_rows_new,

time: 55.5 us -> 51.2 us (0.923)
  blocking collectives: 25.6 us -> 22 us
  starting transfers between devices: 13.4 us -> 15 us
  waiting for transfers between devices: 5.11 us -> 3.97 us
  Pallas kernels: 10.3 us -> 9.18 us
    ppermute x0 -> x3, starting transfers between devices: none -> 8.46 us  [quad(): got[shift] = lax.ppermute(x, axis, [(i, (i + shift) % 4) for i in range(4)])]
    all_to_all x2 -> x1, starting transfers between devices: 13.4 us -> 6.51 us  [exchange(): return lax.all_to_all(x, axes, 0, 0)]
    all_to_all x2, blocking collectives: 25.6 us -> 22 us  [exchange(): return lax.all_to_all(x, axes, 0, 0)]
    all_to_all x2 -> x1, waiting for transfers between devices: 5.11 us -> 2.01 us  [exchange(): return lax.all_to_all(x, axes, 0, 0)]
    ppermute x0 -> x3, waiting for transfers between devices: none -> 1.96 us  [quad(): got[shift] = lax.ppermute(x, axis, [(i, (i + shift) % 4) for i in range(4)])]
    pallas_call x1, Pallas kernels: 0.73 us -> 0.12 us  [shards(): call(lambda *refs: new_rows_kernel(n_col, *refs), [f32(n_row, 8, LANES),...]
  transfers between devices with their start and end apart: 2 -> 4, of which waited for: 2 -> 3; matrix products, arithmetic and copies ran while one was open for 0% -> 0% of each run, Pallas kernels for 8% -> 8%
where the time goes in v3:
time: 51.2 us; the launch traced here: 50.9 us
  blocking collectives  22 us (43%)
  starting transfers between devices  15 us (29%)
  Pallas kernels  9.18 us (18%)
  waiting for transfers between devices  3.97 us (8%)
  between operations  0.76 us (1%)
    all_to_all x2, blocking collectives, exchange(): return lax.all_to_all(x, axes, 0, 0)  22 us
    ppermute x3, starting transfers between devices, quad(): got[shift] = lax.ppermute(x, axis, [(i, (i + shift) % 4) for i in range(4)])  8.46 us
    all_to_all x1, starting transfers between devices, exchange(): return lax.all_to_all(x, axes, 0, 0)  6.51 us
    pallas_call x1, Pallas kernels, shards(): call(rows_kernel, [held[0], held[2], vmem(40, LANES), vmem(40, LANES), vm...  2.81 us
    pallas_call x1, Pallas kernels, shards(): call(load_kernel, [f32(n_row, C_ALL, LANES)] + held, [ANYWHERE] * 3, [WHO...  2.7 us
    pallas_call x1, Pallas kernels, shards(): call(lambda *refs: update_kernel(n_col, *refs), [hbm(*b) for b in blocks]...  2.04 us
    all_to_all x1, waiting for transfers between devices, exchange(): return lax.all_to_all(x, axes, 0, 0)  2.01 us
    ppermute x3, waiting for transfers between devices, quad(): got[shift] = lax.ppermute(x, axis, [(i, (i + shift) % 4) for i in range(4)])  1.96 us
  transfers between devices with their start and end apart: 4, of which 3 were waited for; matrix products, arithmetic and copies ran while one was open for 0% of the time, Pallas kernels for 8%

profile of v3, /device:TPU:1, one launch (start us, length us, event | category | flops | bytes accessed | tf_op | source)
XLA Modules:
  0.0 50.9 jit_solution(7867383690883741626)
XLA Ops:
  0.6 0.0 copy-start
  0.7 0.0 copy-start.1
  0.7 0.0 copy-start.2
  0.7 0.0 copy-start.3
  0.7 0.0 copy-start.4
  0.7 0.0 copy-start.5
  0.7 2.7 %shard_map.187 = (f32[8,16,128]{2,1,0:T(8,128)}, f32[4,512,128]{2,1,0:T(8,128)S(1)}, f32[2,320,512]{2,1,0:T(8,128)S(1)}, f32[1280,128]{1,0:T(8,128)S(1)}) custom-call(f32[4,512,128]{2,1,0:T(8,128)} %a.1, f32[2,320,512]{2,1,0:T(8,128)} %bitcast.9, f32[1280,128]{1,0:T(8,128)} %o.1), custom_call_target="tpu_custom_call" | custom-call | flops 4194304 | bytes 3145728 | tf_op jit(solution)/shard_map/pallas_call | solution.py:370
  3.4 6.5 %all-to-all-start = ((f32[8,16,128]{2,1,0:T(8,128)}), f32[8,16,128]{2,1,0:T(8,128)S(1)}, u32[]{:S(2)}, u32[]{:S(2)}) async-start(f32[8,16,128]{2,1,0:T(8,128)} %get-tuple-element.41), calls=%async_computation | async-start | bytes 131072 | tf_op jit(solution)/shard_map/all_to_all | solution.py:339
  9.9 0.0 copy-done
  9.9 0.0 copy-done.1
  9.9 0.0 copy-done.2
  9.9 0.0 copy-done.3
  10.0 0.0 copy-done.4
  10.0 0.0 copy-done.5
  10.0 2.8 %shard_map.188 = (f32[4,512,128]{2,1,0:T(8,128)S(1)}, f32[1280,128]{1,0:T(8,128)S(1)}, f32[40,128]{1,0:T(8,128)S(1)}, f32[40,128]{1,0:T(8,128)S(1)}, f32[16,128]{1,0:T(8,128)S(1)}) custom-call(f32[4,512,128]{2,1,0:T(8,128)S(1)} %get-tuple-element.35.ga, f32[2,320,512]{2,1,0:T(8,128)S(1)} %get-tuple-element.36.gw, ...), custom_call_target="tpu_custom_call", output_to_operand_aliasing={{0}: (0, {}), {1}: (2, {})} | custom-call | flops 4194304 | bytes 6291456 | tf_op jit(solution)/shard_map/pallas_call | solution.py:380
  12.8 2.0 %all-to-all-done.got = f32[8,16,128]{2,1,0:T(8,128)S(1)} async-done(((f32[8,16,128]{2,1,0:T(8,128)}), f32[8,16,128]{2,1,0:T(8,128)S(1)}, u32[]{:S(2)}, u32[]{:S(2)}) %all-to-all-start) | async-done | bytes 65568 | tf_op jit(solution)/shard_map/all_to_all | solution.py:339
  14.8 0.4 shard_map.189
  15.2 11.2 %all_to_all.15.got = f32[8,72,128]{2,1,0:T(8,128)S(1)} all-to-all(f32[8,72,128]{2,1,0:T(8,128)S(1)} %get-tuple-element.45), channel_id=1, replica_groups=mesh['y'=4,'core'=2,'x'=4,'zq'=4,'zp'=2] {'x','zp'}, dimensions={0} | all-to-all | bytes 589824 | tf_op jit(solution)/shard_map/all_to_all | solution.py:339
  26.4 6.1 %collective-permute-start.2 = (f32[72,128]{1,0:T(8,128)S(1)}, f32[72,128]{1,0:T(8,128)S(1)}, u32[]{:S(2)}, u32[]{:S(2)}) collective-permute-start(f32[72,128]{1,0:T(8,128)S(1)} %shard_map.190.after.refs_2_), channel_id=1, source_target_pairs={{0,4},{2,6},{4,0},{6,2},{1,5},{3,7},{5,1},{7,3},{8,12},{10,14},{12... | collective-permute-start | bytes 110600 | tf_op jit(solution)/shard_map/ppermute | solution.py:345
  32.5 0.3 collective-permute-start.1
  32.7 2.1 %collective-permute-start = (f32[72,128]{1,0:T(8,128)S(1)}, f32[72,128]{1,0:T(8,128)S(1)}, u32[]{:S(2)}, u32[]{:S(2)}) collective-permute-start(f32[72,128]{1,0:T(8,128)S(1)} %shard_map.190.after.refs_2_), channel_id=1, source_target_pairs={{0,2},{2,4},{4,6},{6,0},{1,3},{3,5},{5,7},{7,1},{8,10},{10,12},{12... | collective-permute-start | bytes 110600 | tf_op jit(solution)/shard_map/ppermute | solution.py:345
  34.8 1.1 %shard_map.191 = (f32[4,512,128]{2,1,0:T(8,128)S(1)}, f32[2,320,512]{2,1,0:T(8,128)S(1)}, f32[1280,128]{1,0:T(8,128)S(1)}, f32[4,128]{1,0:T(4,128)}, f32[2,320]{...) custom-call(f32[4,512,128]{2,1,0:T(8,128)S(1)} %get-tuple-element.39, ...), custom_call_target="tpu_custom_call", output_to_operand_aliasing={{0}: (0, {}), {1}: (1, {}), {2}: (2, {})} | custom-call | flops 4194304 | bytes 6291456 | tf_op jit(solution)/shard_map/pallas_call | solution.py:414
  35.9 0.0 collective-permute-done.2.refs_5_
  35.9 1.1 %collective-permute-done.1.refs_4_ = f32[72,128]{1,0:T(8,128)S(1)} collective-permute-done((f32[72,128]{1,0:T(8,128)S(1)}, f32[72,128]{1,0:T(8,128)S(1)}, u32[]{:S(2)}, u32[]{:S(2)}) %collective-permute-start.1) | collective-permute-done | bytes 36896 | tf_op jit(solution)/shard_map/ppermute | solution.py:345
  37.1 0.8 %collective-permute-done.refs_3_ = f32[72,128]{1,0:T(8,128)S(1)} collective-permute-done((f32[72,128]{1,0:T(8,128)S(1)}, f32[72,128]{1,0:T(8,128)S(1)}, u32[]{:S(2)}, u32[]{:S(2)}) %collective-permute-start) | collective-permute-done | bytes 36896 | tf_op jit(solution)/shard_map/ppermute | solution.py:345
  37.9 0.1 shard_map.192
  38.0 10.8 %all_to_all.16.refs_0_ = f32[8,8,128]{2,1,0:T(8,128)S(1)} all-to-all(f32[8,8,128]{2,1,0:T(8,128)S(1)} %get-tuple-element.47), channel_id=1, replica_groups=mesh['y'=4,'core'=2,'x'=4,'zq'=4,'zp'=2] {'y','core'}, dimensions={0} | all-to-all | bytes 65536 | tf_op jit(solution)/shard_map/all_to_all | solution.py:339
  48.8 2.0 %shard_map.193 = (f32[4,512,128]{2,1,0:T(8,128)}, f32[2,320,512]{2,1,0:T(8,128)}, f32[1280,128]{1,0:T(8,128)}, f32[4,512]{1,0:T(4,128)}, f32[2,512]{1,0:T(2,128)}, /*index=5*/f32[10,128]{1,0:T(8,128)}) custom-call(f32[8,8,128]{2,1,0:T(8,128)S(1)} %all_to_all.16.refs_0_, f32[40,128]{1,0:T(8,128)S(1)} %get-tuple-element.48.refs_1_, ...), custom_call_target="tpu_custom_call" | custom-call | flops 4194304 | bytes 3145728 | tf_op jit(solution)/shard_map/pallas_call | solution.py:430
  (1 shorter events, 0.0 us)
Async XLA Ops:
  0.6 9.3 %copy-start = (f32[4,512]{1,0:T(4,128)S(1)}, f32[4,512]{1,0:T(4,128)}, u32[]{:S(2)}) copy-start(f32[4,512]{1,0:T(4,128)} %ar.1) | copy-start | bytes 24580
  0.7 9.3 %copy-start.1 = (f32[1280]{0:T(1024)S(1)}, f32[1280]{0:T(1024)}, u32[]{:S(2)}) copy-start(f32[1280]{0:T(1024)} %param.22) | copy-start | bytes 15364
  0.7 9.3 %copy-start.2 = (f32[2,512]{1,0:T(2,128)S(1)}, f32[2,512]{1,0:T(2,128)}, u32[]{:S(2)}) copy-start(f32[2,512]{1,0:T(2,128)} %wr.1) | copy-start | bytes 12292
  0.7 9.3 %copy-start.3 = (f32[2,320]{1,0:T(2,128)S(1)}, f32[2,320]{1,0:T(2,128)}, u32[]{:S(2)}) copy-start(f32[2,320]{1,0:T(2,128)} %wc.1) | copy-start | bytes 7684
  0.7 9.3 %copy-start.4 = (f32[4,128]{1,0:T(4,128)S(1)}, f32[4,128]{1,0:T(4,128)}, u32[]{:S(2)}) copy-start(f32[4,128]{1,0:T(4,128)} %ac.1) | copy-start | bytes 6148
  0.7 9.3 %copy-start.5 = (f32[128]{0:T(128)S(1)}, f32[128]{0:T(128)}, u32[]{:S(2)}) copy-start(f32[128]{0:T(128)} %param.23) | copy-start | bytes 1540
  3.4 11.4 %all-to-all-start = ((f32[8,16,128]{2,1,0:T(8,128)}), f32[8,16,128]{2,1,0:T(8,128)S(1)}, u32[]{:S(2)}, u32[]{:S(2)}) async-start(f32[8,16,128]{2,1,0:T(8,128)} %get-tuple-element.41), calls=%async_computation | async-start | bytes 131072 | tf_op jit(solution)/shard_map/all_to_all | solution.py:339
  26.4 9.6 %collective-permute-start.2 = (f32[72,128]{1,0:T(8,128)S(1)}, f32[72,128]{1,0:T(8,128)S(1)}, u32[]{:S(2)}, u32[]{:S(2)}) collective-permute-start(f32[72,128]{1,0:T(8,128)S(1)} %shard_map.190.after.refs_2_), channel_id=1, source_target_pairs={{0,4},{2,6},{4,0},{6,2},{1,5},{3,7},{5,1},{7,3},{8,12},{10,14},{12... | collective-permute-start | bytes 110600 | tf_op jit(solution)/shard_map/ppermute | solution.py:345
  32.5 4.6 %collective-permute-start.1 = (f32[72,128]{1,0:T(8,128)S(1)}, f32[72,128]{1,0:T(8,128)S(1)}, u32[]{:S(2)}, u32[]{:S(2)}) collective-permute-start(f32[72,128]{1,0:T(8,128)S(1)} %shard_map.190.after.refs_2_), channel_id=1, source_target_pairs={{0,6},{2,0},{4,2},{6,4},{1,7},{3,1},{5,3},{7,5},{8,14},{10,8},{12,... | collective-permute-start | bytes 110600 | tf_op jit(solution)/shard_map/ppermute | solution.py:345
  32.7 5.1 %collective-permute-start = (f32[72,128]{1,0:T(8,128)S(1)}, f32[72,128]{1,0:T(8,128)S(1)}, u32[]{:S(2)}, u32[]{:S(2)}) collective-permute-start(f32[72,128]{1,0:T(8,128)S(1)} %shard_map.190.after.refs_2_), channel_id=1, source_target_pairs={{0,2},{2,4},{4,6},{6,0},{1,3},{3,5},{5,7},{7,1},{8,10},{10,12},{12... | collective-permute-start | bytes 110600 | tf_op jit(solution)/shard_map/ppermute | solution.py:345

commit v4 on v3

--- a/solution.py
+++ b/solution.py
@@ -13,9 +13,7 @@
 N_MATS = 7
 
 ROW = ("y", "core")
-COL = ("x", "zq", "zp")
-NEAR = ("x", "zp")
-FAR = ("zq",)
+COL = ("x", "z")
 
 A_MATS, A_ROWS = 4, 512
 W_MATS, W_COLS, W_ROWS = 2, 320, 512
@@ -217,20 +215,19 @@
         for t in range(W_TILES):
             at = R_ALL + R_WI + k * W_TILES + t
             packed[at : at + 1, :] = total(sums[t])
-    value = packed[...]
-    for n in range(send.shape[0]):
-        send[n] = value
-
-
-def relay_kernel(got, send):
-    tot = got[0]
-    for n in range(1, got.shape[0]):
-        tot = tot + got[n]
-    send[...] = tot
-
-
-def new_rows_kernel(n_col, old_rows, done, own, before, after, opposite, send, rows, tot, ratio):
-    tot[...] = (own[...] + opposite[...]) + (before[...] + after[...])
+    send[...] = packed[...]
+
+
+def sum4_kernel(own, beside, across, opposite, send):
+    send[...] = (own[...] + opposite[...]) + (across[...] + beside[...])
+
+
+def sum4_and_kernel(done, *refs):
+    sum4_kernel(*refs)
+
+
+def new_rows_kernel(n_col, old_rows, own, other, send, rows, tot, ratio):
+    tot[...] = own[...] + other[...]
     at = lax.broadcasted_iota(jnp.int32, (R_ALL, LANES), 0)
     full_a, full_w = float(LANES * n_col), float(W_COLS * n_col)
     full = jnp.where((at >= R_WI) & (at < R_WO), full_w, full_a)
@@ -339,11 +336,18 @@
     return lax.all_to_all(x, axes, 0, 0)
 
 
-def quad(x, axis, order):
-    got = {0: x}
-    for shift in order:
-        got[shift] = lax.ppermute(x, axis, [(i, (i + shift) % 4) for i in range(4)])
-    return [got[shift] for shift in (0, 1, 3, 2)]
+PAIRINGS = (2, 3, 1)
+
+
+def quad(x, axis):
+    indices = range(lax.axis_size(axis))
+    got = [lax.ppermute(x, axis, [(i, i ^ bits) for i in indices]) for bits in PAIRINGS]
+    return [x] + got[::-1]
+
+
+def mirror(x, axis):
+    n = lax.axis_size(axis)
+    return lax.ppermute(x, axis, [(i, n - 1 - i) for i in range(n)])
 
 
 def shards(
@@ -360,8 +364,7 @@
     wo_rows,
     wo_cols,
 ):
-    n_row, n_near, n_far = (lax.axis_size(axes) for axes in (ROW, NEAR, FAR))
-    n_col = n_near * n_far
+    n_row, n_col = lax.axis_size(ROW), lax.axis_size(COL)
     wi_grad = jnp.swapaxes(wi_grad, 1, 2)
     wi_param = jnp.swapaxes(wi_param, 1, 2)
     blocks = ((A_MATS, A_ROWS, LANES), (W_MATS, W_COLS, W_ROWS), (O_ROWS, LANES))
@@ -402,15 +405,15 @@
     ta, to = here(ta), here(to)
     send, cols = call(
         cols_kernel,
-        [f32(n_near, S_ALL, LANES), vmem(C_ALL, LANES)],
+        [f32(S_ALL, LANES), vmem(C_ALL, LANES)],
         [WHOLE] * 6,
         [WHOLE] * 2,
         [vmem(S_ALL, LANES)],
         bytes_accessed=3 << 20,
     )(got, here(old_cols), here(row_sums), ta, gw, to)
-    got = exchange(send, NEAR)
-    send = call(relay_kernel, f32(S_ALL, LANES), [WHOLE], WHOLE)(got)
-    got = quad(send, "zq", (1, 3, 2))
+    got = quad(send, "x")
+    send = call(sum4_kernel, f32(S_ALL, LANES), [WHOLE] * 4, WHOLE)(*got)
+    got = quad(send, "z")
     ua, uw, uo, attn_cols_new, wi_cols_new, wo_cols_new, done = call(
         scaled_kernel,
         held + [f32(A_MATS, LANES), f32(W_MATS, W_COLS), f32(1, LANES), vmem(8, LANES)],
@@ -419,13 +422,15 @@
         bytes_accessed=6 << 20,
         aliases={0: 0, 1: 1, 2: 2},
     )(ta, gw, to, here(cols), send)
+    send = call(sum4_and_kernel, f32(S_ALL, LANES), [ANYWHERE] + [WHOLE] * 4, WHOLE)(here(done), *got)
+    got = mirror(send, "z")
     send, rows = call(
         lambda *refs: new_rows_kernel(n_col, *refs),
         [f32(n_row, 8, LANES), vmem(40, LANES)],
-        [WHOLE, ANYWHERE] + [WHOLE] * 4,
+        [WHOLE] * 3,
         [WHOLE] * 2,
         [vmem(S_ALL, LANES), vmem(R_ALL, LANES)],
-    )(here(old_rows), here(done), *got)
+    )(here(old_rows), send, got)
     got = exchange(send, ROW)
     attn_update, wi_update, wo_update, attn_rows_new, wi_rows_new, wo_rows_new = call(
         lambda *refs: update_kernel(n_col, *refs),
@@ -449,7 +454,7 @@
 
 
 def solution(mesh):
-    fine = Mesh(mesh.devices.reshape(4, 2, 4, 4, 2), ROW + COL)
+    fine = Mesh(mesh.devices.reshape(4, 2, 4, 8), ROW + COL)
     big, row, col = P(None, ROW, COL), P(None, ROW), P(None, COL)
     return jax.shard_map(
         shards,

time: 51.2 us -> 48.8 us (0.953)
  blocking collectives: 22 us -> 11.2 us
  waiting for transfers between devices: 3.97 us -> 8.45 us
  starting transfers between devices: 15 us -> 19 us
    all_to_all x2 -> x1, blocking collectives: 22 us -> 11.2 us  [exchange(): return lax.all_to_all(x, axes, 0, 0)]
    ppermute x3 -> x7, waiting for transfers between devices: 1.96 us -> 6.44 us  [the longest x6 5.09 us: quad(): lax.ppermute(x, axis, [(i, i ^ bits) for i in indices])]
    ppermute x3 -> x7, starting transfers between devices: 8.46 us -> 12.5 us  [the longest x6 7.87 us: quad(): lax.ppermute(x, axis, [(i, i ^ bits) for i in indices])]
  transfers between devices with their start and end apart: 4 -> 8, of which waited for: 3 -> 5; matrix products, arithmetic and copies ran while one was open for 0% -> 0% of each run, Pallas kernels for 8% -> 8%
where the time goes in v4:
time: 48.8 us; the launch traced here: 48.5 us
  starting transfers between devices  19 us (39%)
  blocking collectives  11.2 us (23%)
  Pallas kernels  9.17 us (19%)
  waiting for transfers between devices  8.45 us (17%)
  between operations  0.77 us (2%)
    all_to_all x1, blocking collectives, exchange(): return lax.all_to_all(x, axes, 0, 0)  11.2 us
    ppermute x6, starting transfers between devices, quad(): lax.ppermute(x, axis, [(i, i ^ bits) for i in indices])  7.87 us
    all_to_all x1, starting transfers between devices, exchange(): return lax.all_to_all(x, axes, 0, 0)  6.51 us
    ppermute x6, waiting for transfers between devices, quad(): lax.ppermute(x, axis, [(i, i ^ bits) for i in indices])  5.09 us
    ppermute x1, starting transfers between devices, mirror(): return lax.ppermute(x, axis, [(i, n - 1 - i) for i in range(n)])  4.62 us
    pallas_call x1, Pallas kernels, shards(): call(rows_kernel, [held[0], held[2], vmem(40, LANES), vmem(40, LANES), vm...  2.81 us
    pallas_call x1, Pallas kernels, shards(): call(load_kernel, [f32(n_row, C_ALL, LANES)] + held, [ANYWHERE] * 3, [WHO...  2.7 us
    pallas_call x1, Pallas kernels, shards(): call(lambda *refs: update_kernel(n_col, *refs), [hbm(*b) for b in blocks]...  2.04 us
  transfers between devices with their start and end apart: 8, of which 5 were waited for; matrix products, arithmetic and copies ran while one was open for 0% of the time, Pallas kernels for 8%

profile of v4, /device:TPU:1, one launch (start us, length us, event | category | flops | bytes accessed | tf_op | source)
XLA Modules:
  0.0 48.5 jit_solution(5495735830026703951)
XLA Ops:
  0.6 0.0 copy-start
  0.7 0.0 copy-start.1
  0.7 0.0 copy-start.2
  0.7 0.0 copy-start.3
  0.7 2.7 %shard_map.187 = (f32[8,16,128]{2,1,0:T(8,128)}, f32[4,512,128]{2,1,0:T(8,128)S(1)}, f32[2,320,512]{2,1,0:T(8,128)S(1)}, f32[1280,128]{1,0:T(8,128)S(1)}) custom-call(f32[4,512,128]{2,1,0:T(8,128)} %a.1, f32[2,320,512]{2,1,0:T(8,128)} %bitcast.9, f32[1280,128]{1,0:T(8,128)} %o.1), custom_call_target="tpu_custom_call" | custom-call | flops 4194304 | bytes 3145728 | tf_op jit(solution)/shard_map/pallas_call | solution.py:373
  3.4 6.5 %all-to-all-start = ((f32[8,16,128]{2,1,0:T(8,128)}), f32[8,16,128]{2,1,0:T(8,128)S(1)}, u32[]{:S(2)}, u32[]{:S(2)}) async-start(f32[8,16,128]{2,1,0:T(8,128)} %get-tuple-element.41), calls=%async_computation | async-start | bytes 131072 | tf_op jit(solution)/shard_map/all_to_all | solution.py:336
  9.9 0.0 copy-done.1
  9.9 0.0 copy-done.2
  9.9 0.0 copy-done.3
  10.0 0.0 copy-done.4
  10.0 0.0 copy-done.5
  10.0 2.8 %shard_map.188 = (f32[4,512,128]{2,1,0:T(8,128)S(1)}, f32[1280,128]{1,0:T(8,128)S(1)}, f32[40,128]{1,0:T(8,128)S(1)}, f32[40,128]{1,0:T(8,128)S(1)}, f32[16,128]{1,0:T(8,128)S(1)}) custom-call(f32[4,512,128]{2,1,0:T(8,128)S(1)} %get-tuple-element.35.ga, f32[2,320,512]{2,1,0:T(8,128)S(1)} %get-tuple-element.36.gw, ...), custom_call_target="tpu_custom_call", output_to_operand_aliasing={{0}: (0, {}), {1}: (2, {})} | custom-call | flops 4194304 | bytes 6291456 | tf_op jit(solution)/shard_map/pallas_call | solution.py:383
  12.8 2.0 %all-to-all-done.got = f32[8,16,128]{2,1,0:T(8,128)S(1)} async-done(((f32[8,16,128]{2,1,0:T(8,128)}), f32[8,16,128]{2,1,0:T(8,128)S(1)}, u32[]{:S(2)}, u32[]{:S(2)}) %all-to-all-start) | async-done | bytes 65568 | tf_op jit(solution)/shard_map/all_to_all | solution.py:336
  14.8 0.4 shard_map.189
  15.2 2.3 %collective-permute-start.2 = (f32[72,128]{1,0:T(8,128)S(1)}, f32[72,128]{1,0:T(8,128)S(1)}, u32[]{:S(2)}, u32[]{:S(2)}) collective-permute-start(f32[72,128]{1,0:T(8,128)S(1)} %get-tuple-element.45.own), channel_id=1, source_target_pairs={{0,16},{8,24},{16,0},{24,8},{1,17},{9,25},{17,1},{25,9},{2,18},{10... | collective-permute-start | bytes 110600 | tf_op jit(solution)/shard_map/ppermute | solution.py:344
  17.5 0.9 %collective-permute-start.1 = (f32[72,128]{1,0:T(8,128)S(1)}, f32[72,128]{1,0:T(8,128)S(1)}, u32[]{:S(2)}, u32[]{:S(2)}) collective-permute-start(f32[72,128]{1,0:T(8,128)S(1)} %get-tuple-element.45.own), channel_id=1, source_target_pairs={{0,24},{8,16},{16,8},{24,0},{1,25},{9,17},{17,9},{25,1},{2,26},{10... | collective-permute-start | bytes 110600 | tf_op jit(solution)/shard_map/ppermute | solution.py:344
  18.3 0.0 collective-permute-start
  18.3 1.2 %collective-permute-done.2.opposite = f32[72,128]{1,0:T(8,128)S(1)} collective-permute-done((f32[72,128]{1,0:T(8,128)S(1)}, f32[72,128]{1,0:T(8,128)S(1)}, u32[]{:S(2)}, u32[]{:S(2)}) %collective-permute-start.2) | collective-permute-done | bytes 36896 | tf_op jit(solution)/shard_map/ppermute | solution.py:344
  19.6 1.9 %collective-permute-done.1.across = f32[72,128]{1,0:T(8,128)S(1)} collective-permute-done((f32[72,128]{1,0:T(8,128)S(1)}, f32[72,128]{1,0:T(8,128)S(1)}, u32[]{:S(2)}, u32[]{:S(2)}) %collective-permute-start.1) | collective-permute-done | bytes 36896 | tf_op jit(solution)/shard_map/ppermute | solution.py:344
  21.5 0.0 collective-permute-done.beside
  21.5 3.1 %collective-permute-start.5 = (f32[72,128]{1,0:T(8,128)S(1)}, f32[72,128]{1,0:T(8,128)S(1)}, u32[]{:S(2)}, u32[]{:S(2)}) collective-permute-start(f32[72,128]{1,0:T(8,128)S(1)} %shard_map.190.after.refs_0_), channel_id=1, source_target_pairs={{0,2},{1,3},{2,0},{3,1},{4,6},{5,7},{6,4},{7,5},{8,10},{9,11},{10,... | collective-permute-start | bytes 110600 | tf_op jit(solution)/shard_map/ppermute | solution.py:344
  24.6 1.5 %collective-permute-start.4 = (f32[72,128]{1,0:T(8,128)S(1)}, f32[72,128]{1,0:T(8,128)S(1)}, u32[]{:S(2)}, u32[]{:S(2)}) collective-permute-start(f32[72,128]{1,0:T(8,128)S(1)} %shard_map.190.after.refs_0_), channel_id=1, source_target_pairs={{0,3},{1,2},{2,1},{3,0},{4,7},{5,6},{6,5},{7,4},{8,11},{9,10},{10,... | collective-permute-start | bytes 110600 | tf_op jit(solution)/shard_map/ppermute | solution.py:344
  26.1 0.2 collective-permute-start.3
  26.2 1.1 %shard_map.191 = (f32[4,512,128]{2,1,0:T(8,128)S(1)}, f32[2,320,512]{2,1,0:T(8,128)S(1)}, f32[1280,128]{1,0:T(8,128)S(1)}, f32[4,128]{1,0:T(4,128)}, f32[2,320]{...) custom-call(f32[4,512,128]{2,1,0:T(8,128)S(1)} %get-tuple-element.39, ...), custom_call_target="tpu_custom_call", output_to_operand_aliasing={{0}: (0, {}), {1}: (1, {}), {2}: (2, {})} | custom-call | flops 4194304 | bytes 6291456 | tf_op jit(solution)/shard_map/pallas_call | solution.py:417
  27.3 0.0 collective-permute-done.5.refs_3_
  27.3 1.9 %collective-permute-done.4.refs_2_ = f32[72,128]{1,0:T(8,128)S(1)} collective-permute-done((f32[72,128]{1,0:T(8,128)S(1)}, f32[72,128]{1,0:T(8,128)S(1)}, u32[]{:S(2)}, u32[]{:S(2)}) %collective-permute-start.4) | collective-permute-done | bytes 36896 | tf_op jit(solution)/shard_map/ppermute | solution.py:344
  29.3 0.0 collective-permute-done.3.refs_1_
  29.3 4.6 %collective-permute-start.6 = (f32[72,128]{1,0:T(8,128)S(1)}, f32[72,128]{1,0:T(8,128)S(1)}, u32[]{:S(2)}, u32[]{:S(2)}) collective-permute-start(f32[72,128]{1,0:T(8,128)S(1)} %shard_map.192.refs_1_), channel_id=1, source_target_pairs={{0,7},{1,6},{2,5},{3,4},{4,3},{5,2},{6,1},{7,0},{8,15},{9,14},{10,... | collective-permute-start | bytes 110600 | tf_op jit(solution)/shard_map/ppermute | solution.py:350
  33.9 1.3 %collective-permute-done.6.refs_2_ = f32[72,128]{1,0:T(8,128)S(1)} collective-permute-done((f32[72,128]{1,0:T(8,128)S(1)}, f32[72,128]{1,0:T(8,128)S(1)}, u32[]{:S(2)}, u32[]{:S(2)}) %collective-permute-start.6) | collective-permute-done | bytes 36896 | tf_op jit(solution)/shard_map/ppermute | solution.py:350
  35.2 0.1 shard_map.193
  35.4 11.2 %all_to_all.10.refs_0_ = f32[8,8,128]{2,1,0:T(8,128)S(1)} all-to-all(f32[8,8,128]{2,1,0:T(8,128)S(1)} %get-tuple-element.47), channel_id=1, replica_groups=mesh['y'=4,'core'=2,'x'=4,'z'=8] {'y','core'}, dimensions={0} | all-to-all | bytes 65536 | tf_op jit(solution)/shard_map/all_to_all | solution.py:336
  46.5 2.0 %shard_map.194 = (f32[4,512,128]{2,1,0:T(8,128)}, f32[2,320,512]{2,1,0:T(8,128)}, f32[1280,128]{1,0:T(8,128)}, f32[4,512]{1,0:T(4,128)}, f32[2,512]{1,0:T(2,128)}, /*index=5*/f32[10,128]{1,0:T(8,128)}) custom-call(f32[8,8,128]{2,1,0:T(8,128)S(1)} %all_to_all.10.refs_0_, f32[40,128]{1,0:T(8,128)S(1)} %get-tuple-element.48.refs_1_, ...), custom_call_target="tpu_custom_call" | custom-call | flops 4194304 | bytes 3145728 | tf_op jit(solution)/shard_map/pallas_call | solution.py:435
  (5 shorter events, 0.0 us)
Async XLA Ops:
  0.6 9.3 %copy-start = (f32[4,512]{1,0:T(4,128)S(1)}, f32[4,512]{1,0:T(4,128)}, u32[]{:S(2)}) copy-start(f32[4,512]{1,0:T(4,128)} %ar.1) | copy-start | bytes 24580
  0.7 9.3 %copy-start.1 = (f32[1280]{0:T(1024)S(1)}, f32[1280]{0:T(1024)}, u32[]{:S(2)}) copy-start(f32[1280]{0:T(1024)} %param.22) | copy-start | bytes 15364
  0.7 9.3 %copy-start.2 = (f32[2,512]{1,0:T(2,128)S(1)}, f32[2,512]{1,0:T(2,128)}, u32[]{:S(2)}) copy-start(f32[2,512]{1,0:T(2,128)} %wr.1) | copy-start | bytes 12292
  0.7 9.3 %copy-start.3 = (f32[2,320]{1,0:T(2,128)S(1)}, f32[2,320]{1,0:T(2,128)}, u32[]{:S(2)}) copy-start(f32[2,320]{1,0:T(2,128)} %wc.1) | copy-start | bytes 7684
  0.7 9.3 %copy-start.4 = (f32[4,128]{1,0:T(4,128)S(1)}, f32[4,128]{1,0:T(4,128)}, u32[]{:S(2)}) copy-start(f32[4,128]{1,0:T(4,128)} %ac.1) | copy-start | bytes 6148
  0.7 9.3 %copy-start.5 = (f32[128]{0:T(128)S(1)}, f32[128]{0:T(128)}, u32[]{:S(2)}) copy-start(f32[128]{0:T(128)} %param.23) | copy-start | bytes 1540
  3.4 11.4 %all-to-all-start = ((f32[8,16,128]{2,1,0:T(8,128)}), f32[8,16,128]{2,1,0:T(8,128)S(1)}, u32[]{:S(2)}, u32[]{:S(2)}) async-start(f32[8,16,128]{2,1,0:T(8,128)} %get-tuple-element.41), calls=%async_computation | async-start | bytes 131072 | tf_op jit(solution)/shard_map/all_to_all | solution.py:336
  15.2 4.4 %collective-permute-start.2 = (f32[72,128]{1,0:T(8,128)S(1)}, f32[72,128]{1,0:T(8,128)S(1)}, u32[]{:S(2)}, u32[]{:S(2)}) collective-permute-start(f32[72,128]{1,0:T(8,128)S(1)} %get-tuple-element.45.own), channel_id=1, source_target_pairs={{0,16},{8,24},{16,0},{24,8},{1,17},{9,25},{17,1},{25,9},{2,18},{10... | collective-permute-start | bytes 110600 | tf_op jit(solution)/shard_map/ppermute | solution.py:344
  17.5 4.0 %collective-permute-start.1 = (f32[72,128]{1,0:T(8,128)S(1)}, f32[72,128]{1,0:T(8,128)S(1)}, u32[]{:S(2)}, u32[]{:S(2)}) collective-permute-start(f32[72,128]{1,0:T(8,128)S(1)} %get-tuple-element.45.own), channel_id=1, source_target_pairs={{0,24},{8,16},{16,8},{24,0},{1,25},{9,17},{17,9},{25,1},{2,26},{10... | collective-permute-start | bytes 110600 | tf_op jit(solution)/shard_map/ppermute | solution.py:344
  18.3 3.2 %collective-permute-start = (f32[72,128]{1,0:T(8,128)S(1)}, f32[72,128]{1,0:T(8,128)S(1)}, u32[]{:S(2)}, u32[]{:S(2)}) collective-permute-start(f32[72,128]{1,0:T(8,128)S(1)} %get-tuple-element.45.own), channel_id=1, source_target_pairs={{0,8},{8,0},{16,24},{24,16},{1,9},{9,1},{17,25},{25,17},{2,10},{10... | collective-permute-start | bytes 110600 | tf_op jit(solution)/shard_map/ppermute | solution.py:344
  21.5 5.8 %collective-permute-start.5 = (f32[72,128]{1,0:T(8,128)S(1)}, f32[72,128]{1,0:T(8,128)S(1)}, u32[]{:S(2)}, u32[]{:S(2)}) collective-permute-start(f32[72,128]{1,0:T(8,128)S(1)} %shard_map.190.after.refs_0_), channel_id=1, source_target_pairs={{0,2},{1,3},{2,0},{3,1},{4,6},{5,7},{6,4},{7,5},{8,10},{9,11},{10,... | collective-permute-start | bytes 110600 | tf_op jit(solution)/shard_map/ppermute | solution.py:344
  24.6 4.7 %collective-permute-start.4 = (f32[72,128]{1,0:T(8,128)S(1)}, f32[72,128]{1,0:T(8,128)S(1)}, u32[]{:S(2)}, u32[]{:S(2)}) collective-permute-start(f32[72,128]{1,0:T(8,128)S(1)} %shard_map.190.after.refs_0_), channel_id=1, source_target_pairs={{0,3},{1,2},{2,1},{3,0},{4,7},{5,6},{6,5},{7,4},{8,11},{9,10},{10,... | collective-permute-start | bytes 110600 | tf_op jit(solution)/shard_map/ppermute | solution.py:344
  26.1 3.2 %collective-permute-start.3 = (f32[72,128]{1,0:T(8,128)S(1)}, f32[72,128]{1,0:T(8,128)S(1)}, u32[]{:S(2)}, u32[]{:S(2)}) collective-permute-start(f32[72,128]{1,0:T(8,128)S(1)} %shard_map.190.after.refs_0_), channel_id=1, source_target_pairs={{0,1},{1,0},{2,3},{3,2},{4,5},{5,4},{6,7},{7,6},{8,9},{9,8},{10,11... | collective-permute-start | bytes 110600 | tf_op jit(solution)/shard_map/ppermute | solution.py:344
  29.3 6.0 %collective-permute-start.6 = (f32[72,128]{1,0:T(8,128)S(1)}, f32[72,128]{1,0:T(8,128)S(1)}, u32[]{:S(2)}, u32[]{:S(2)}) collective-permute-start(f32[72,128]{1,0:T(8,128)S(1)} %shard_map.192.refs_1_), channel_id=1, source_target_pairs={{0,7},{1,6},{2,5},{3,4},{4,3},{5,2},{6,1},{7,0},{8,15},{9,14},{10,... | collective-permute-start | bytes 110600 | tf_op jit(solution)/shard_map/ppermute | solution.py:350

commit v5 on v4

--- a/solution.py
+++ b/solution.py
@@ -218,8 +218,8 @@
     send[...] = packed[...]
 
 
-def sum4_kernel(own, beside, across, opposite, send):
-    send[...] = (own[...] + opposite[...]) + (across[...] + beside[...])
+def sum4_kernel(own, third, second, first, send):
+    send[...] = (own[...] + first[...]) + (second[...] + third[...])
 
 
 def sum4_and_kernel(done, *refs):
@@ -249,7 +249,11 @@
     levels = jnp.sum(levels, axis=1, keepdims=True)
     ratios = jnp.sum(ratios, axis=1, keepdims=True)
     params = jnp.sum(params, axis=1, keepdims=True)
-    value = jnp.where(lane < 32, levels, jnp.where(lane < 64, ratios, params))
+    value = total(
+        jnp.where(lane == sub, levels, 0.0)
+        + jnp.where(lane == sub + 32, ratios, 0.0)
+        + jnp.where(lane == sub + 64, params, 0.0)
+    )
     for n in range(send.shape[0]):
         send[n] = value
 
@@ -293,15 +297,20 @@
     tot = got[0]
     for n in range(1, got.shape[0]):
         tot = tot + got[n]
+    sub = lax.broadcasted_iota(jnp.int32, (8, LANES), 0)
+    lane = lax.broadcasted_iota(jnp.int32, (8, LANES), 1)
+    levels, ratios, params = (
+        jnp.sum(jnp.where(lane == sub + at, tot, 0.0), axis=1, keepdims=True) for at in (0, 32, 64)
+    )
     sub = lax.broadcasted_iota(jnp.int32, (8, 1), 0)
     n_row = got.shape[0]
     full_rows = jnp.where(sub == N_MATS - 1, float(O_ROWS * n_row), float(A_ROWS * n_row))
     wide = (sub >= A_MATS) & (sub < A_MATS + W_MATS)
     full_cols = jnp.where(wide, float(W_COLS * n_col), float(LANES * n_col))
     count = full_rows * full_cols
-    level = tot[:, 0:1] / full_rows
-    dir_rms = jnp.sqrt(level * tot[:, 32:33] / count)
-    param_rms = jnp.sqrt(tot[:, 64:65] / count)
+    level = levels / full_rows
+    dir_rms = jnp.sqrt(level * ratios / count)
+    param_rms = jnp.sqrt(params / count)
     factor = -RHO * param_rms / jnp.maximum(1.0, dir_rms) * jnp.sqrt(level)
     for k in range(W_MATS):
         f = factor[A_MATS + k : A_MATS + k + 1, :]
@@ -336,12 +345,9 @@
     return lax.all_to_all(x, axes, 0, 0)
 
 
-PAIRINGS = (2, 3, 1)
-
-
-def quad(x, axis):
+def quad(x, axis, pairings):
     indices = range(lax.axis_size(axis))
-    got = [lax.ppermute(x, axis, [(i, i ^ bits) for i in indices]) for bits in PAIRINGS]
+    got = [lax.ppermute(x, axis, [(i, i ^ bits) for i in indices]) for bits in pairings]
     return [x] + got[::-1]
 
 
@@ -411,9 +417,9 @@
         [vmem(S_ALL, LANES)],
         bytes_accessed=3 << 20,
     )(got, here(old_cols), here(row_sums), ta, gw, to)
-    got = quad(send, "x")
+    got = quad(send, "z", (3, 2, 1))
     send = call(sum4_kernel, f32(S_ALL, LANES), [WHOLE] * 4, WHOLE)(*got)
-    got = quad(send, "z")
+    got = quad(send, "x", (2, 3, 1))
     ua, uw, uo, attn_cols_new, wi_cols_new, wo_cols_new, done = call(
         scaled_kernel,
         held + [f32(A_MATS, LANES), f32(W_MATS, W_COLS), f32(1, LANES), vmem(8, LANES)],
@@ -426,7 +432,7 @@
     got = mirror(send, "z")
     send, rows = call(
         lambda *refs: new_rows_kernel(n_col, *refs),
-        [f32(n_row, 8, LANES), vmem(40, LANES)],
+        [f32(n_row, 1, LANES), vmem(40, LANES)],
         [WHOLE] * 3,
         [WHOLE] * 2,
         [vmem(S_ALL, LANES), vmem(R_ALL, LANES)],

time: 48.8 us -> 47.8 us (0.980)
  starting transfers between devices: 19 us -> 17.7 us
  waiting for transfers between devices: 8.45 us -> 9.36 us
  blocking collectives: 11.2 us -> 10.6 us
    ppermute x1, starting transfers between devices: 4.62 us -> 3.24 us  [mirror(): return lax.ppermute(x, axis, [(i, n - 1 - i) for i in range(n)])]
    ppermute x6, waiting for transfers between devices: 5.09 us -> 6.01 us  [quad(): lax.ppermute(x, axis, [(i, i ^ bits) for i in indices])]
    all_to_all x1, blocking collectives: 11.2 us -> 10.6 us  [exchange(): return lax.all_to_all(x, axes, 0, 0)]
where the time goes in v5:
time: 47.8 us; the launch traced here: 47.6 us
  starting transfers between devices  17.7 us (37%)
  blocking collectives  10.6 us (22%)
  waiting for transfers between devices  9.36 us (20%)
  Pallas kernels  9.06 us (19%)
  between operations  0.77 us (2%)
    all_to_all x1, blocking collectives, exchange(): return lax.all_to_all(x, axes, 0, 0)  10.6 us
    ppermute x6, starting transfers between devices, quad(): lax.ppermute(x, axis, [(i, i ^ bits) for i in indices])  7.97 us
    all_to_all x1, starting transfers between devices, exchange(): return lax.all_to_all(x, axes, 0, 0)  6.51 us
    ppermute x6, waiting for transfers between devices, quad(): lax.ppermute(x, axis, [(i, i ^ bits) for i in indices])  6.01 us
    ppermute x1, starting transfers between devices, mirror(): return lax.ppermute(x, axis, [(i, n - 1 - i) for i in range(n)])  3.24 us
    pallas_call x1, Pallas kernels, shards(): call(rows_kernel, [held[0], held[2], vmem(40, LANES), vmem(40, LANES), vm...  2.81 us
    pallas_call x1, Pallas kernels, shards(): call(load_kernel, [f32(n_row, C_ALL, LANES)] + held, [ANYWHERE] * 3, [WHO...  2.7 us
    all_to_all x1, waiting for transfers between devices, exchange(): return lax.all_to_all(x, axes, 0, 0)  2.01 us
  transfers between devices with their start and end apart: 8, of which 5 were waited for; matrix products, arithmetic and copies ran while one was open for 0% of the time, Pallas kernels for 8%

profile of v5, /device:TPU:1, one launch (start us, length us, event | category | flops | bytes accessed | tf_op | source)
XLA Modules:
  0.0 47.6 jit_solution(7139708885259073616)
XLA Ops:
  0.6 0.0 copy-start
  0.7 0.0 copy-start.1
  0.7 0.0 copy-start.2
  0.7 0.0 copy-start.3
  0.7 0.0 copy-start.4
  0.7 0.0 copy-start.5
  0.7 2.7 %shard_map.187 = (f32[8,16,128]{2,1,0:T(8,128)}, f32[4,512,128]{2,1,0:T(8,128)S(1)}, f32[2,320,512]{2,1,0:T(8,128)S(1)}, f32[1280,128]{1,0:T(8,128)S(1)}) custom-call(f32[4,512,128]{2,1,0:T(8,128)} %a.1, f32[2,320,512]{2,1,0:T(8,128)} %bitcast.9, f32[1280,128]{1,0:T(8,128)} %o.1), custom_call_target="tpu_custom_call" | custom-call | flops 4194304 | bytes 3145728 | tf_op jit(solution)/shard_map/pallas_call | solution.py:379
  3.4 6.5 %all-to-all-start = ((f32[8,16,128]{2,1,0:T(8,128)}), f32[8,16,128]{2,1,0:T(8,128)S(1)}, u32[]{:S(2)}, u32[]{:S(2)}) async-start(f32[8,16,128]{2,1,0:T(8,128)} %get-tuple-element.41), calls=%async_computation | async-start | bytes 131072 | tf_op jit(solution)/shard_map/all_to_all | solution.py:345
  9.9 0.0 copy-done
  9.9 0.0 copy-done.1
  9.9 0.0 copy-done.2
  10.0 2.8 %shard_map.188 = (f32[4,512,128]{2,1,0:T(8,128)S(1)}, f32[1280,128]{1,0:T(8,128)S(1)}, f32[40,128]{1,0:T(8,128)S(1)}, f32[40,128]{1,0:T(8,128)S(1)}, f32[16,128]{1,0:T(8,128)S(1)}) custom-call(f32[4,512,128]{2,1,0:T(8,128)S(1)} %get-tuple-element.35.ga, f32[2,320,512]{2,1,0:T(8,128)S(1)} %get-tuple-element.36.gw, ...), custom_call_target="tpu_custom_call", output_to_operand_aliasing={{0}: (0, {}), {1}: (2, {})} | custom-call | flops 4194304 | bytes 6291456 | tf_op jit(solution)/shard_map/pallas_call | solution.py:389
  12.8 2.0 %all-to-all-done.got = f32[8,16,128]{2,1,0:T(8,128)S(1)} async-done(((f32[8,16,128]{2,1,0:T(8,128)}), f32[8,16,128]{2,1,0:T(8,128)S(1)}, u32[]{:S(2)}, u32[]{:S(2)}) %all-to-all-start) | async-done | bytes 65568 | tf_op jit(solution)/shard_map/all_to_all | solution.py:345
  14.8 0.4 shard_map.189
  15.2 3.9 %collective-permute-start.2 = (f32[72,128]{1,0:T(8,128)S(1)}, f32[72,128]{1,0:T(8,128)S(1)}, u32[]{:S(2)}, u32[]{:S(2)}) collective-permute-start(f32[72,128]{1,0:T(8,128)S(1)} %get-tuple-element.45.own), channel_id=1, source_target_pairs={{0,3},{1,2},{2,1},{3,0},{4,7},{5,6},{6,5},{7,4},{8,11},{9,10},{10,... | collective-permute-start | bytes 110600 | tf_op jit(solution)/shard_map/ppermute | solution.py:350
  19.1 0.0 collective-permute-start.1
  19.1 0.4 collective-permute-start
  19.5 1.1 %collective-permute-done.2.first = f32[72,128]{1,0:T(8,128)S(1)} collective-permute-done((f32[72,128]{1,0:T(8,128)S(1)}, f32[72,128]{1,0:T(8,128)S(1)}, u32[]{:S(2)}, u32[]{:S(2)}) %collective-permute-start.2) | collective-permute-done | bytes 36896 | tf_op jit(solution)/shard_map/ppermute | solution.py:350
  20.5 2.8 %collective-permute-done.1.second = f32[72,128]{1,0:T(8,128)S(1)} collective-permute-done((f32[72,128]{1,0:T(8,128)S(1)}, f32[72,128]{1,0:T(8,128)S(1)}, u32[]{:S(2)}, u32[]{:S(2)}) %collective-permute-start.1) | collective-permute-done | bytes 36896 | tf_op jit(solution)/shard_map/ppermute | solution.py:350
  23.3 0.0 collective-permute-done.third
  23.3 2.8 %collective-permute-start.5 = (f32[72,128]{1,0:T(8,128)S(1)}, f32[72,128]{1,0:T(8,128)S(1)}, u32[]{:S(2)}, u32[]{:S(2)}) collective-permute-start(f32[72,128]{1,0:T(8,128)S(1)} %shard_map.190.after.refs_0_), channel_id=1, source_target_pairs={{0,16},{8,24},{16,0},{24,8},{1,17},{9,25},{17,1},{25,9},{2,18},{10... | collective-permute-start | bytes 110600 | tf_op jit(solution)/shard_map/ppermute | solution.py:350
  26.1 0.9 %collective-permute-start.4 = (f32[72,128]{1,0:T(8,128)S(1)}, f32[72,128]{1,0:T(8,128)S(1)}, u32[]{:S(2)}, u32[]{:S(2)}) collective-permute-start(f32[72,128]{1,0:T(8,128)S(1)} %shard_map.190.after.refs_0_), channel_id=1, source_target_pairs={{0,24},{8,16},{16,8},{24,0},{1,25},{9,17},{17,9},{25,1},{2,26},{10... | collective-permute-start | bytes 110600 | tf_op jit(solution)/shard_map/ppermute | solution.py:350
  27.0 0.0 collective-permute-start.3
  27.0 1.1 %shard_map.191 = (f32[4,512,128]{2,1,0:T(8,128)S(1)}, f32[2,320,512]{2,1,0:T(8,128)S(1)}, f32[1280,128]{1,0:T(8,128)S(1)}, f32[4,128]{1,0:T(4,128)}, f32[2,320]{...) custom-call(f32[4,512,128]{2,1,0:T(8,128)S(1)} %get-tuple-element.39, ...), custom_call_target="tpu_custom_call", output_to_operand_aliasing={{0}: (0, {}), {1}: (1, {}), {2}: (2, {})} | custom-call | flops 4194304 | bytes 6291456 | tf_op jit(solution)/shard_map/pallas_call | solution.py:423
  28.1 0.0 collective-permute-done.5.refs_3_
  28.1 2.2 %collective-permute-done.4.refs_2_ = f32[72,128]{1,0:T(8,128)S(1)} collective-permute-done((f32[72,128]{1,0:T(8,128)S(1)}, f32[72,128]{1,0:T(8,128)S(1)}, u32[]{:S(2)}, u32[]{:S(2)}) %collective-permute-start.4) | collective-permute-done | bytes 36896 | tf_op jit(solution)/shard_map/ppermute | solution.py:350
  30.3 0.0 collective-permute-done.3.refs_1_
  30.3 3.2 %collective-permute-start.6 = (f32[72,128]{1,0:T(8,128)S(1)}, f32[72,128]{1,0:T(8,128)S(1)}, u32[]{:S(2)}, u32[]{:S(2)}) collective-permute-start(f32[72,128]{1,0:T(8,128)S(1)} %shard_map.192.refs_1_), channel_id=1, source_target_pairs={{0,7},{1,6},{2,5},{3,4},{4,3},{5,2},{6,1},{7,0},{8,15},{9,14},{10,... | collective-permute-start | bytes 110600 | tf_op jit(solution)/shard_map/ppermute | solution.py:356
  33.5 1.3 %collective-permute-done.6.refs_2_ = f32[72,128]{1,0:T(8,128)S(1)} collective-permute-done((f32[72,128]{1,0:T(8,128)S(1)}, f32[72,128]{1,0:T(8,128)S(1)}, u32[]{:S(2)}, u32[]{:S(2)}) %collective-permute-start.6) | collective-permute-done | bytes 36896 | tf_op jit(solution)/shard_map/ppermute | solution.py:356
  34.9 0.1 shard_map.193
  35.0 10.6 %all_to_all.10.refs_0_ = f32[8,1,128]{2,1,0:T(1,128)S(1)} all-to-all(f32[8,1,128]{2,1,0:T(1,128)S(1)} %get-tuple-element.47), channel_id=1, replica_groups=mesh['y'=4,'core'=2,'x'=4,'z'=8] {'y','core'}, dimensions={0} | all-to-all | bytes 8192 | tf_op jit(solution)/shard_map/all_to_all | solution.py:345
  45.6 1.9 %shard_map.194 = (f32[4,512,128]{2,1,0:T(8,128)}, f32[2,320,512]{2,1,0:T(8,128)}, f32[1280,128]{1,0:T(8,128)}, f32[4,512]{1,0:T(4,128)}, f32[2,512]{1,0:T(2,128)}, /*index=5*/f32[10,128]{1,0:T(8,128)}) custom-call(f32[8,1,128]{2,1,0:T(1,128)S(1)} %all_to_all.10.refs_0_, f32[40,128]{1,0:T(8,128)S(1)} %get-tuple-element.48.refs_1_, ...), custom_call_target="tpu_custom_call" | custom-call | flops 4194304 | bytes 3145728 | tf_op jit(solution)/shard_map/pallas_call | solution.py:441
  (5 shorter events, 0.0 us)
Async XLA Ops:
  0.6 9.3 %copy-start = (f32[4,512]{1,0:T(4,128)S(1)}, f32[4,512]{1,0:T(4,128)}, u32[]{:S(2)}) copy-start(f32[4,512]{1,0:T(4,128)} %ar.1) | copy-start | bytes 24580
  0.7 9.3 %copy-start.1 = (f32[1280]{0:T(1024)S(1)}, f32[1280]{0:T(1024)}, u32[]{:S(2)}) copy-start(f32[1280]{0:T(1024)} %param.22) | copy-start | bytes 15364
  0.7 9.3 %copy-start.2 = (f32[2,512]{1,0:T(2,128)S(1)}, f32[2,512]{1,0:T(2,128)}, u32[]{:S(2)}) copy-start(f32[2,512]{1,0:T(2,128)} %wr.1) | copy-start | bytes 12292
  0.7 9.3 %copy-start.3 = (f32[2,320]{1,0:T(2,128)S(1)}, f32[2,320]{1,0:T(2,128)}, u32[]{:S(2)}) copy-start(f32[2,320]{1,0:T(2,128)} %wc.1) | copy-start | bytes 7684
  0.7 9.3 %copy-start.4 = (f32[4,128]{1,0:T(4,128)S(1)}, f32[4,128]{1,0:T(4,128)}, u32[]{:S(2)}) copy-start(f32[4,128]{1,0:T(4,128)} %ac.1) | copy-start | bytes 6148
  0.7 9.3 %copy-start.5 = (f32[128]{0:T(128)S(1)}, f32[128]{0:T(128)}, u32[]{:S(2)}) copy-start(f32[128]{0:T(128)} %param.23) | copy-start | bytes 1540
  3.4 11.4 %all-to-all-start = ((f32[8,16,128]{2,1,0:T(8,128)}), f32[8,16,128]{2,1,0:T(8,128)S(1)}, u32[]{:S(2)}, u32[]{:S(2)}) async-start(f32[8,16,128]{2,1,0:T(8,128)} %get-tuple-element.41), calls=%async_computation | async-start | bytes 131072 | tf_op jit(solution)/shard_map/all_to_all | solution.py:345
  15.2 5.3 %collective-permute-start.2 = (f32[72,128]{1,0:T(8,128)S(1)}, f32[72,128]{1,0:T(8,128)S(1)}, u32[]{:S(2)}, u32[]{:S(2)}) collective-permute-start(f32[72,128]{1,0:T(8,128)S(1)} %get-tuple-element.45.own), channel_id=1, source_target_pairs={{0,3},{1,2},{2,1},{3,0},{4,7},{5,6},{6,5},{7,4},{8,11},{9,10},{10,... | collective-permute-start | bytes 110600 | tf_op jit(solution)/shard_map/ppermute | solution.py:350
  19.1 4.2 %collective-permute-start.1 = (f32[72,128]{1,0:T(8,128)S(1)}, f32[72,128]{1,0:T(8,128)S(1)}, u32[]{:S(2)}, u32[]{:S(2)}) collective-permute-start(f32[72,128]{1,0:T(8,128)S(1)} %get-tuple-element.45.own), channel_id=1, source_target_pairs={{0,2},{1,3},{2,0},{3,1},{4,6},{5,7},{6,4},{7,5},{8,10},{9,11},{10,... | collective-permute-start | bytes 110600 | tf_op jit(solution)/shard_map/ppermute | solution.py:350
  19.1 4.2 %collective-permute-start = (f32[72,128]{1,0:T(8,128)S(1)}, f32[72,128]{1,0:T(8,128)S(1)}, u32[]{:S(2)}, u32[]{:S(2)}) collective-permute-start(f32[72,128]{1,0:T(8,128)S(1)} %get-tuple-element.45.own), channel_id=1, source_target_pairs={{0,1},{1,0},{2,3},{3,2},{4,5},{5,4},{6,7},{7,6},{8,9},{9,8},{10,11... | collective-permute-start | bytes 110600 | tf_op jit(solution)/shard_map/ppermute | solution.py:350
  23.3 4.8 %collective-permute-start.5 = (f32[72,128]{1,0:T(8,128)S(1)}, f32[72,128]{1,0:T(8,128)S(1)}, u32[]{:S(2)}, u32[]{:S(2)}) collective-permute-start(f32[72,128]{1,0:T(8,128)S(1)} %shard_map.190.after.refs_0_), channel_id=1, source_target_pairs={{0,16},{8,24},{16,0},{24,8},{1,17},{9,25},{17,1},{25,9},{2,18},{10... | collective-permute-start | bytes 110600 | tf_op jit(solution)/shard_map/ppermute | solution.py:350
  26.1 4.1 %collective-permute-start.4 = (f32[72,128]{1,0:T(8,128)S(1)}, f32[72,128]{1,0:T(8,128)S(1)}, u32[]{:S(2)}, u32[]{:S(2)}) collective-permute-start(f32[72,128]{1,0:T(8,128)S(1)} %shard_map.190.after.refs_0_), channel_id=1, source_target_pairs={{0,24},{8,16},{16,8},{24,0},{1,25},{9,17},{17,9},{25,1},{2,26},{10... | collective-permute-start | bytes 110600 | tf_op jit(solution)/shard_map/ppermute | solution.py:350
  27.0 3.3 %collective-permute-start.3 = (f32[72,128]{1,0:T(8,128)S(1)}, f32[72,128]{1,0:T(8,128)S(1)}, u32[]{:S(2)}, u32[]{:S(2)}) collective-permute-start(f32[72,128]{1,0:T(8,128)S(1)} %shard_map.190.after.refs_0_), channel_id=1, source_target_pairs={{0,8},{8,0},{16,24},{24,16},{1,9},{9,1},{17,25},{25,17},{2,10},{10... | collective-permute-start | bytes 110600 | tf_op jit(solution)/shard_map/ppermute | solution.py:350
  30.3 4.6 %collective-permute-start.6 = (f32[72,128]{1,0:T(8,128)S(1)}, f32[72,128]{1,0:T(8,128)S(1)}, u32[]{:S(2)}, u32[]{:S(2)}) collective-permute-start(f32[72,128]{1,0:T(8,128)S(1)} %shard_map.192.refs_1_), channel_id=1, source_target_pairs={{0,7},{1,6},{2,5},{3,4},{4,3},{5,2},{6,1},{7,0},{8,15},{9,14},{10,... | collective-permute-start | bytes 110600 | tf_op jit(solution)/shard_map/ppermute | solution.py:356

commit v6 on v5

--- a/solution.py
+++ b/solution.py
@@ -21,7 +21,7 @@
 A_TILES, O_TILES, W_TILES = A_ROWS // LANES, O_ROWS // LANES, W_ROWS // LANES
 W_COL_TILES = -(-W_COLS // LANES)
 
-C_WI, C_WO, C_ALL = 4, 10, 16
+C_WI, C_WO, C_SENT, C_ALL = 4, 10, 11, 16
 R_WI, R_WO, R_ALL = 16, 24, 34
 S_PARAM, S_ALL = 2 * R_ALL, 72
 
@@ -106,9 +106,10 @@
     copies[-1].wait()
     g = go[...]
     packed[C_WO : C_WO + 1, :] = total(g * g + EPS_SQUARE)
-    value = packed[...]
-    for n in range(send.shape[0]):
-        send[n] = value
+    for i in range(C_SENT):
+        row = packed[i : i + 1, :]
+        for n in range(send.shape[0]):
+            send[n, :, i * LANES : (i + 1) * LANES] = row
 
 
 def wi_places():
@@ -180,9 +181,13 @@
 
 
 def cols_kernel(got, old_cols, row_sums, ta, gw, to, send, cols, packed):
-    tot = got[0]
+    flat = got[0]
     for n in range(1, got.shape[0]):
-        tot = tot + got[n]
+        flat = flat + got[n]
+    cols[...] = jnp.zeros_like(cols)
+    for i in range(C_SENT):
+        cols[i : i + 1, :] = flat[:, i * LANES : (i + 1) * LANES]
+    tot = cols[...]
     at = lax.broadcasted_iota(jnp.int32, (C_ALL, LANES), 0)
     full_a, full_o = float(A_ROWS * got.shape[0]), float(O_ROWS * got.shape[0])
     mean = tot / jnp.where(at == C_WO, full_o, full_a)
@@ -378,7 +383,7 @@
     sems = pltpu.SemaphoreType.DMA((N_MATS,))
     send, ga, gw, go = call(
         load_kernel,
-        [f32(n_row, C_ALL, LANES)] + held,
+        [f32(n_row, 1, C_SENT * LANES)] + held,
         [ANYWHERE] * 3,
         [WHOLE] * 4,
         [vmem(C_ALL, LANES), sems],

time: 47.8 us -> 47.7 us (level)
  no operation moved by 1% of the time
where the time goes in v6:
time: 47.7 us; the launch traced here: 47.5 us
  starting transfers between devices  17.7 us (37%)
  blocking collectives  10.6 us (22%)
  waiting for transfers between devices  9.25 us (19%)
  Pallas kernels  9.06 us (19%)
  between operations  0.77 us (2%)
    all_to_all x1, blocking collectives, exchange(): return lax.all_to_all(x, axes, 0, 0)  10.6 us
    ppermute x6, starting transfers between devices, quad(): lax.ppermute(x, axis, [(i, i ^ bits) for i in indices])  7.97 us
    all_to_all x1, starting transfers between devices, exchange(): return lax.all_to_all(x, axes, 0, 0)  6.5 us
    ppermute x6, waiting for transfers between devices, quad(): lax.ppermute(x, axis, [(i, i ^ bits) for i in indices])  5.98 us
    ppermute x1, starting transfers between devices, mirror(): return lax.ppermute(x, axis, [(i, n - 1 - i) for i in range(n)])  3.27 us
    pallas_call x1, Pallas kernels, shards(): call(rows_kernel, [held[0], held[2], vmem(40, LANES), vmem(40, LANES), vm...  2.81 us
    pallas_call x1, Pallas kernels, shards(): call(load_kernel, [f32(n_row, 1, C_SENT * LANES)] + held, [ANYWHERE] * 3,...  2.69 us
    all_to_all x1, waiting for transfers between devices, exchange(): return lax.all_to_all(x, axes, 0, 0)  1.92 us
  transfers between devices with their start and end apart: 8, of which 5 were waited for; matrix products, arithmetic and copies ran while one was open for 0% of the time, Pallas kernels for 8%

profile of v6, /device:TPU:1, one launch (start us, length us, event | category | flops | bytes accessed | tf_op | source)
XLA Modules:
  0.0 47.5 jit_solution(10163428798738919284)
XLA Ops:
  0.6 0.0 copy-start
  0.7 0.0 copy-start.1
  0.7 0.0 copy-start.2
  0.7 0.0 copy-start.3
  0.7 0.0 copy-start.4
  0.7 0.0 copy-start.5
  0.7 2.7 %shard_map.187 = (f32[8,1,1408]{2,1,0:T(1,128)}, f32[4,512,128]{2,1,0:T(8,128)S(1)}, f32[2,320,512]{2,1,0:T(8,128)S(1)}, f32[1280,128]{1,0:T(8,128)S(1)}) custom-call(f32[4,512,128]{2,1,0:T(8,128)} %a.1, f32[2,320,512]{2,1,0:T(8,128)} %bitcast.9, f32[1280,128]{1,0:T(8,128)} %o.1), custom_call_target="tpu_custom_call" | custom-call | flops 4194304 | bytes 3145728 | tf_op jit(solution)/shard_map/pallas_call | solution.py:384
  3.4 6.5 %all-to-all-start = ((f32[8,1,1408]{2,1,0:T(1,128)}), f32[8,1,1408]{2,1,0:T(1,128)S(1)}, u32[]{:S(2)}, u32[]{:S(2)}) async-start(f32[8,1,1408]{2,1,0:T(1,128)} %get-tuple-element.41), calls=%async_computation | async-start | bytes 90112 | tf_op jit(solution)/shard_map/all_to_all | solution.py:350
  9.9 0.0 copy-done
  9.9 0.0 copy-done.1
  9.9 0.0 copy-done.2
  10.0 2.8 %shard_map.188 = (f32[4,512,128]{2,1,0:T(8,128)S(1)}, f32[1280,128]{1,0:T(8,128)S(1)}, f32[40,128]{1,0:T(8,128)S(1)}, f32[40,128]{1,0:T(8,128)S(1)}, f32[16,128]{1,0:T(8,128)S(1)}) custom-call(f32[4,512,128]{2,1,0:T(8,128)S(1)} %get-tuple-element.35.ga, f32[2,320,512]{2,1,0:T(8,128)S(1)} %get-tuple-element.36.gw, ...), custom_call_target="tpu_custom_call", output_to_operand_aliasing={{0}: (0, {}), {1}: (2, {})} | custom-call | flops 4194304 | bytes 6291456 | tf_op jit(solution)/shard_map/pallas_call | solution.py:394
  12.8 1.9 %all-to-all-done.got = f32[8,1,1408]{2,1,0:T(1,128)S(1)} async-done(((f32[8,1,1408]{2,1,0:T(1,128)}), f32[8,1,1408]{2,1,0:T(1,128)S(1)}, u32[]{:S(2)}, u32[]{:S(2)}) %all-to-all-start) | async-done | bytes 45088 | tf_op jit(solution)/shard_map/all_to_all | solution.py:350
  14.7 0.4 shard_map.189
  15.1 3.9 %collective-permute-start.2 = (f32[72,128]{1,0:T(8,128)S(1)}, f32[72,128]{1,0:T(8,128)S(1)}, u32[]{:S(2)}, u32[]{:S(2)}) collective-permute-start(f32[72,128]{1,0:T(8,128)S(1)} %get-tuple-element.45.own), channel_id=1, source_target_pairs={{0,3},{1,2},{2,1},{3,0},{4,7},{5,6},{6,5},{7,4},{8,11},{9,10},{10,... | collective-permute-start | bytes 110600 | tf_op jit(solution)/shard_map/ppermute | solution.py:355
  19.0 0.0 collective-permute-start.1
  19.0 0.4 collective-permute-start
  19.4 1.0 %collective-permute-done.2.first = f32[72,128]{1,0:T(8,128)S(1)} collective-permute-done((f32[72,128]{1,0:T(8,128)S(1)}, f32[72,128]{1,0:T(8,128)S(1)}, u32[]{:S(2)}, u32[]{:S(2)}) %collective-permute-start.2) | collective-permute-done | bytes 36896 | tf_op jit(solution)/shard_map/ppermute | solution.py:355
  20.4 2.8 %collective-permute-done.1.second = f32[72,128]{1,0:T(8,128)S(1)} collective-permute-done((f32[72,128]{1,0:T(8,128)S(1)}, f32[72,128]{1,0:T(8,128)S(1)}, u32[]{:S(2)}, u32[]{:S(2)}) %collective-permute-start.1) | collective-permute-done | bytes 36896 | tf_op jit(solution)/shard_map/ppermute | solution.py:355
  23.2 0.0 collective-permute-done.third
  23.2 2.8 %collective-permute-start.5 = (f32[72,128]{1,0:T(8,128)S(1)}, f32[72,128]{1,0:T(8,128)S(1)}, u32[]{:S(2)}, u32[]{:S(2)}) collective-permute-start(f32[72,128]{1,0:T(8,128)S(1)} %shard_map.190.after.refs_0_), channel_id=1, source_target_pairs={{0,16},{8,24},{16,0},{24,8},{1,17},{9,25},{17,1},{25,9},{2,18},{10... | collective-permute-start | bytes 110600 | tf_op jit(solution)/shard_map/ppermute | solution.py:355
  26.1 0.9 %collective-permute-start.4 = (f32[72,128]{1,0:T(8,128)S(1)}, f32[72,128]{1,0:T(8,128)S(1)}, u32[]{:S(2)}, u32[]{:S(2)}) collective-permute-start(f32[72,128]{1,0:T(8,128)S(1)} %shard_map.190.after.refs_0_), channel_id=1, source_target_pairs={{0,24},{8,16},{16,8},{24,0},{1,25},{9,17},{17,9},{25,1},{2,26},{10... | collective-permute-start | bytes 110600 | tf_op jit(solution)/shard_map/ppermute | solution.py:355
  26.9 0.0 collective-permute-start.3
  26.9 1.1 %shard_map.191 = (f32[4,512,128]{2,1,0:T(8,128)S(1)}, f32[2,320,512]{2,1,0:T(8,128)S(1)}, f32[1280,128]{1,0:T(8,128)S(1)}, f32[4,128]{1,0:T(4,128)}, f32[2,320]{...) custom-call(f32[4,512,128]{2,1,0:T(8,128)S(1)} %get-tuple-element.39, ...), custom_call_target="tpu_custom_call", output_to_operand_aliasing={{0}: (0, {}), {1}: (1, {}), {2}: (2, {})} | custom-call | flops 4194304 | bytes 6291456 | tf_op jit(solution)/shard_map/pallas_call | solution.py:428
  28.0 0.0 collective-permute-done.5.refs_3_
  28.0 2.1 %collective-permute-done.4.refs_2_ = f32[72,128]{1,0:T(8,128)S(1)} collective-permute-done((f32[72,128]{1,0:T(8,128)S(1)}, f32[72,128]{1,0:T(8,128)S(1)}, u32[]{:S(2)}, u32[]{:S(2)}) %collective-permute-start.4) | collective-permute-done | bytes 36896 | tf_op jit(solution)/shard_map/ppermute | solution.py:355
  30.2 0.0 collective-permute-done.3.refs_1_
  30.2 3.3 %collective-permute-start.6 = (f32[72,128]{1,0:T(8,128)S(1)}, f32[72,128]{1,0:T(8,128)S(1)}, u32[]{:S(2)}, u32[]{:S(2)}) collective-permute-start(f32[72,128]{1,0:T(8,128)S(1)} %shard_map.192.refs_1_), channel_id=1, source_target_pairs={{0,7},{1,6},{2,5},{3,4},{4,3},{5,2},{6,1},{7,0},{8,15},{9,14},{10,... | collective-permute-start | bytes 110600 | tf_op jit(solution)/shard_map/ppermute | solution.py:361
  33.5 1.3 %collective-permute-done.6.refs_2_ = f32[72,128]{1,0:T(8,128)S(1)} collective-permute-done((f32[72,128]{1,0:T(8,128)S(1)}, f32[72,128]{1,0:T(8,128)S(1)}, u32[]{:S(2)}, u32[]{:S(2)}) %collective-permute-start.6) | collective-permute-done | bytes 36896 | tf_op jit(solution)/shard_map/ppermute | solution.py:361
  34.8 0.1 shard_map.193
  34.9 10.6 %all_to_all.10.refs_0_ = f32[8,1,128]{2,1,0:T(1,128)S(1)} all-to-all(f32[8,1,128]{2,1,0:T(1,128)S(1)} %get-tuple-element.47), channel_id=1, replica_groups=mesh['y'=4,'core'=2,'x'=4,'z'=8] {'y','core'}, dimensions={0} | all-to-all | bytes 8192 | tf_op jit(solution)/shard_map/all_to_all | solution.py:350
  45.5 1.9 %shard_map.194 = (f32[4,512,128]{2,1,0:T(8,128)}, f32[2,320,512]{2,1,0:T(8,128)}, f32[1280,128]{1,0:T(8,128)}, f32[4,512]{1,0:T(4,128)}, f32[2,512]{1,0:T(2,128)}, /*index=5*/f32[10,128]{1,0:T(8,128)}) custom-call(f32[8,1,128]{2,1,0:T(1,128)S(1)} %all_to_all.10.refs_0_, f32[40,128]{1,0:T(8,128)S(1)} %get-tuple-element.48.refs_1_, ...), custom_call_target="tpu_custom_call" | custom-call | flops 4194304 | bytes 3145728 | tf_op jit(solution)/shard_map/pallas_call | solution.py:446
  (5 shorter events, 0.0 us)
Async XLA Ops:
  0.6 9.3 %copy-start = (f32[4,512]{1,0:T(4,128)S(1)}, f32[4,512]{1,0:T(4,128)}, u32[]{:S(2)}) copy-start(f32[4,512]{1,0:T(4,128)} %ar.1) | copy-start | bytes 24580
  0.7 9.3 %copy-start.1 = (f32[1280]{0:T(1024)S(1)}, f32[1280]{0:T(1024)}, u32[]{:S(2)}) copy-start(f32[1280]{0:T(1024)} %param.22) | copy-start | bytes 15364
  0.7 9.3 %copy-start.2 = (f32[2,512]{1,0:T(2,128)S(1)}, f32[2,512]{1,0:T(2,128)}, u32[]{:S(2)}) copy-start(f32[2,512]{1,0:T(2,128)} %wr.1) | copy-start | bytes 12292
  0.7 9.3 %copy-start.3 = (f32[2,320]{1,0:T(2,128)S(1)}, f32[2,320]{1,0:T(2,128)}, u32[]{:S(2)}) copy-start(f32[2,320]{1,0:T(2,128)} %wc.1) | copy-start | bytes 7684
  0.7 9.3 %copy-start.4 = (f32[4,128]{1,0:T(4,128)S(1)}, f32[4,128]{1,0:T(4,128)}, u32[]{:S(2)}) copy-start(f32[4,128]{1,0:T(4,128)} %ac.1) | copy-start | bytes 6148
  0.7 9.3 %copy-start.5 = (f32[128]{0:T(128)S(1)}, f32[128]{0:T(128)}, u32[]{:S(2)}) copy-start(f32[128]{0:T(128)} %param.23) | copy-start | bytes 1540
  3.4 11.3 %all-to-all-start = ((f32[8,1,1408]{2,1,0:T(1,128)}), f32[8,1,1408]{2,1,0:T(1,128)S(1)}, u32[]{:S(2)}, u32[]{:S(2)}) async-start(f32[8,1,1408]{2,1,0:T(1,128)} %get-tuple-element.41), calls=%async_computation | async-start | bytes 90112 | tf_op jit(solution)/shard_map/all_to_all | solution.py:350
  15.1 5.3 %collective-permute-start.2 = (f32[72,128]{1,0:T(8,128)S(1)}, f32[72,128]{1,0:T(8,128)S(1)}, u32[]{:S(2)}, u32[]{:S(2)}) collective-permute-start(f32[72,128]{1,0:T(8,128)S(1)} %get-tuple-element.45.own), channel_id=1, source_target_pairs={{0,3},{1,2},{2,1},{3,0},{4,7},{5,6},{6,5},{7,4},{8,11},{9,10},{10,... | collective-permute-start | bytes 110600 | tf_op jit(solution)/shard_map/ppermute | solution.py:355
  19.0 4.2 %collective-permute-start.1 = (f32[72,128]{1,0:T(8,128)S(1)}, f32[72,128]{1,0:T(8,128)S(1)}, u32[]{:S(2)}, u32[]{:S(2)}) collective-permute-start(f32[72,128]{1,0:T(8,128)S(1)} %get-tuple-element.45.own), channel_id=1, source_target_pairs={{0,2},{1,3},{2,0},{3,1},{4,6},{5,7},{6,4},{7,5},{8,10},{9,11},{10,... | collective-permute-start | bytes 110600 | tf_op jit(solution)/shard_map/ppermute | solution.py:355
  19.0 4.2 %collective-permute-start = (f32[72,128]{1,0:T(8,128)S(1)}, f32[72,128]{1,0:T(8,128)S(1)}, u32[]{:S(2)}, u32[]{:S(2)}) collective-permute-start(f32[72,128]{1,0:T(8,128)S(1)} %get-tuple-element.45.own), channel_id=1, source_target_pairs={{0,1},{1,0},{2,3},{3,2},{4,5},{5,4},{6,7},{7,6},{8,9},{9,8},{10,11... | collective-permute-start | bytes 110600 | tf_op jit(solution)/shard_map/ppermute | solution.py:355
  23.2 4.8 %collective-permute-start.5 = (f32[72,128]{1,0:T(8,128)S(1)}, f32[72,128]{1,0:T(8,128)S(1)}, u32[]{:S(2)}, u32[]{:S(2)}) collective-permute-start(f32[72,128]{1,0:T(8,128)S(1)} %shard_map.190.after.refs_0_), channel_id=1, source_target_pairs={{0,16},{8,24},{16,0},{24,8},{1,17},{9,25},{17,1},{25,9},{2,18},{10... | collective-permute-start | bytes 110600 | tf_op jit(solution)/shard_map/ppermute | solution.py:355
  26.1 4.1 %collective-permute-start.4 = (f32[72,128]{1,0:T(8,128)S(1)}, f32[72,128]{1,0:T(8,128)S(1)}, u32[]{:S(2)}, u32[]{:S(2)}) collective-permute-start(f32[72,128]{1,0:T(8,128)S(1)} %shard_map.190.after.refs_0_), channel_id=1, source_target_pairs={{0,24},{8,16},{16,8},{24,0},{1,25},{9,17},{17,9},{25,1},{2,26},{10... | collective-permute-start | bytes 110600 | tf_op jit(solution)/shard_map/ppermute | solution.py:355
  26.9 3.2 %collective-permute-start.3 = (f32[72,128]{1,0:T(8,128)S(1)}, f32[72,128]{1,0:T(8,128)S(1)}, u32[]{:S(2)}, u32[]{:S(2)}) collective-permute-start(f32[72,128]{1,0:T(8,128)S(1)} %shard_map.190.after.refs_0_), channel_id=1, source_target_pairs={{0,8},{8,0},{16,24},{24,16},{1,9},{9,1},{17,25},{25,17},{2,10},{10... | collective-permute-start | bytes 110600 | tf_op jit(solution)/shard_map/ppermute | solution.py:355
  30.2 4.6 %collective-permute-start.6 = (f32[72,128]{1,0:T(8,128)S(1)}, f32[72,128]{1,0:T(8,128)S(1)}, u32[]{:S(2)}, u32[]{:S(2)}) collective-permute-start(f32[72,128]{1,0:T(8,128)S(1)} %shard_map.192.refs_1_), channel_id=1, source_target_pairs={{0,7},{1,6},{2,5},{3,4},{4,3},{5,2},{6,1},{7,0},{8,15},{9,14},{10,... | collective-permute-start | bytes 110600 | tf_op jit(solution)/shard_map/ppermute | solution.py:361

commit v7 on v6

--- a/solution.py
+++ b/solution.py
@@ -389,7 +389,7 @@
         [vmem(C_ALL, LANES), sems],
         bytes_accessed=3 << 20,
     )(far(attn_grad), far(wi_grad), far(wo_grad))
-    got = exchange(send, ROW)
+    got = exchange(send, ROW[::-1])
     ga, gw, go = here(ga), here(gw), here(go)
     ta, to, row_sums, old_rows, old_cols = call(
         rows_kernel,
@@ -442,7 +442,7 @@
         [WHOLE] * 2,
         [vmem(S_ALL, LANES), vmem(R_ALL, LANES)],
     )(here(old_rows), send, got)
-    got = exchange(send, ROW)
+    got = exchange(send, ROW[::-1])
     attn_update, wi_update, wo_update, attn_rows_new, wi_rows_new, wo_rows_new = call(
         lambda *refs: update_kernel(n_col, *refs),
         [hbm(*b) for b in blocks] + [hbm(A_MATS, A_ROWS), hbm(W_MATS, W_ROWS), hbm(O_TILES, LANES)],

time: 47.7 us -> 47.6 us (level)
  blocking collectives: 10.6 us -> 9.62 us
  starting transfers between devices: 17.7 us -> 18.5 us
    all_to_all x1, blocking collectives: 10.6 us -> 9.62 us  [exchange(): return lax.all_to_all(x, axes, 0, 0)]
    ppermute x1, starting transfers between devices: 3.27 us -> 3.98 us  [mirror(): return lax.ppermute(x, axis, [(i, n - 1 - i) for i in range(n)])]
where the time goes in v7:
time: 47.6 us; the launch traced here: 47.4 us
  starting transfers between devices  18.5 us (39%)
  blocking collectives  9.62 us (20%)
  waiting for transfers between devices  9.41 us (20%)
  Pallas kernels  9.06 us (19%)
  between operations  0.77 us (2%)
    all_to_all x1, blocking collectives, exchange(): return lax.all_to_all(x, axes, 0, 0)  9.62 us
    ppermute x6, starting transfers between devices, quad(): lax.ppermute(x, axis, [(i, i ^ bits) for i in indices])  7.98 us
    all_to_all x1, starting transfers between devices, exchange(): return lax.all_to_all(x, axes, 0, 0)  6.52 us
    ppermute x6, waiting for transfers between devices, quad(): lax.ppermute(x, axis, [(i, i ^ bits) for i in indices])  5.63 us
    ppermute x1, starting transfers between devices, mirror(): return lax.ppermute(x, axis, [(i, n - 1 - i) for i in range(n)])  3.98 us
    pallas_call x1, Pallas kernels, shards(): call(rows_kernel, [held[0], held[2], vmem(40, LANES), vmem(40, LANES), vm...  2.81 us
    pallas_call x1, Pallas kernels, shards(): call(load_kernel, [f32(n_row, 1, C_SENT * LANES)] + held, [ANYWHERE] * 3,...  2.69 us
    all_to_all x1, waiting for transfers between devices, exchange(): return lax.all_to_all(x, axes, 0, 0)  2.06 us
  transfers between devices with their start and end apart: 8, of which 5 were waited for; matrix products, arithmetic and copies ran while one was open for 0% of the time, Pallas kernels for 8%

profile of v7, /device:TPU:1, one launch (start us, length us, event | category | flops | bytes accessed | tf_op | source)
XLA Modules:
  0.0 47.4 jit_solution(8001874660206098255)
XLA Ops:
  0.6 0.0 copy-start
  0.7 0.0 copy-start.1
  0.7 0.0 copy-start.2
  0.7 0.0 copy-start.3
  0.7 0.0 copy-start.4
  0.7 0.0 copy-start.5
  0.7 2.7 %shard_map.187 = (f32[8,1,1408]{2,1,0:T(1,128)}, f32[4,512,128]{2,1,0:T(8,128)S(1)}, f32[2,320,512]{2,1,0:T(8,128)S(1)}, f32[1280,128]{1,0:T(8,128)S(1)}) custom-call(f32[4,512,128]{2,1,0:T(8,128)} %a.1, f32[2,320,512]{2,1,0:T(8,128)} %bitcast.9, f32[1280,128]{1,0:T(8,128)} %o.1), custom_call_target="tpu_custom_call" | custom-call | flops 4194304 | bytes 3145728 | tf_op jit(solution)/shard_map/pallas_call | solution.py:384
  3.4 6.5 %all-to-all-start = ((f32[8,1,1408]{2,1,0:T(1,128)}), f32[8,1,1408]{2,1,0:T(1,128)S(1)}, u32[]{:S(2)}, u32[]{:S(2)}) async-start(f32[8,1,1408]{2,1,0:T(1,128)} %get-tuple-element.41), calls=%async_computation | async-start | bytes 90112 | tf_op jit(solution)/shard_map/all_to_all | solution.py:350
  9.9 0.0 copy-done
  9.9 0.0 copy-done.1
  9.9 0.0 copy-done.2
  10.0 2.8 %shard_map.188 = (f32[4,512,128]{2,1,0:T(8,128)S(1)}, f32[1280,128]{1,0:T(8,128)S(1)}, f32[40,128]{1,0:T(8,128)S(1)}, f32[40,128]{1,0:T(8,128)S(1)}, f32[16,128]{1,0:T(8,128)S(1)}) custom-call(f32[4,512,128]{2,1,0:T(8,128)S(1)} %get-tuple-element.35.ga, f32[2,320,512]{2,1,0:T(8,128)S(1)} %get-tuple-element.36.gw, ...), custom_call_target="tpu_custom_call", output_to_operand_aliasing={{0}: (0, {}), {1}: (2, {})} | custom-call | flops 4194304 | bytes 6291456 | tf_op jit(solution)/shard_map/pallas_call | solution.py:394
  12.8 2.1 %all-to-all-done.got = f32[8,1,1408]{2,1,0:T(1,128)S(1)} async-done(((f32[8,1,1408]{2,1,0:T(1,128)}), f32[8,1,1408]{2,1,0:T(1,128)S(1)}, u32[]{:S(2)}, u32[]{:S(2)}) %all-to-all-start) | async-done | bytes 45088 | tf_op jit(solution)/shard_map/all_to_all | solution.py:350
  14.9 0.4 shard_map.189
  15.3 3.9 %collective-permute-start.2 = (f32[72,128]{1,0:T(8,128)S(1)}, f32[72,128]{1,0:T(8,128)S(1)}, u32[]{:S(2)}, u32[]{:S(2)}) collective-permute-start(f32[72,128]{1,0:T(8,128)S(1)} %get-tuple-element.45.own), channel_id=1, source_target_pairs={{0,3},{1,2},{2,1},{3,0},{4,7},{5,6},{6,5},{7,4},{8,11},{9,10},{10,... | collective-permute-start | bytes 110600 | tf_op jit(solution)/shard_map/ppermute | solution.py:355
  19.2 0.0 collective-permute-start.1
  19.2 0.4 collective-permute-start
  19.6 1.0 %collective-permute-done.2.first = f32[72,128]{1,0:T(8,128)S(1)} collective-permute-done((f32[72,128]{1,0:T(8,128)S(1)}, f32[72,128]{1,0:T(8,128)S(1)}, u32[]{:S(2)}, u32[]{:S(2)}) %collective-permute-start.2) | collective-permute-done | bytes 36896 | tf_op jit(solution)/shard_map/ppermute | solution.py:355
  20.5 2.6 %collective-permute-done.1.second = f32[72,128]{1,0:T(8,128)S(1)} collective-permute-done((f32[72,128]{1,0:T(8,128)S(1)}, f32[72,128]{1,0:T(8,128)S(1)}, u32[]{:S(2)}, u32[]{:S(2)}) %collective-permute-start.1) | collective-permute-done | bytes 36896 | tf_op jit(solution)/shard_map/ppermute | solution.py:355
  23.1 0.0 collective-permute-done.third
  23.1 2.8 %collective-permute-start.5 = (f32[72,128]{1,0:T(8,128)S(1)}, f32[72,128]{1,0:T(8,128)S(1)}, u32[]{:S(2)}, u32[]{:S(2)}) collective-permute-start(f32[72,128]{1,0:T(8,128)S(1)} %shard_map.190.after.refs_0_), channel_id=1, source_target_pairs={{0,16},{8,24},{16,0},{24,8},{1,17},{9,25},{17,1},{25,9},{2,18},{10... | collective-permute-start | bytes 110600 | tf_op jit(solution)/shard_map/ppermute | solution.py:355
  25.9 0.9 %collective-permute-start.4 = (f32[72,128]{1,0:T(8,128)S(1)}, f32[72,128]{1,0:T(8,128)S(1)}, u32[]{:S(2)}, u32[]{:S(2)}) collective-permute-start(f32[72,128]{1,0:T(8,128)S(1)} %shard_map.190.after.refs_0_), channel_id=1, source_target_pairs={{0,24},{8,16},{16,8},{24,0},{1,25},{9,17},{17,9},{25,1},{2,26},{10... | collective-permute-start | bytes 110600 | tf_op jit(solution)/shard_map/ppermute | solution.py:355
  26.8 0.0 collective-permute-start.3
  26.8 1.1 %shard_map.191 = (f32[4,512,128]{2,1,0:T(8,128)S(1)}, f32[2,320,512]{2,1,0:T(8,128)S(1)}, f32[1280,128]{1,0:T(8,128)S(1)}, f32[4,128]{1,0:T(4,128)}, f32[2,320]{...) custom-call(f32[4,512,128]{2,1,0:T(8,128)S(1)} %get-tuple-element.39, ...), custom_call_target="tpu_custom_call", output_to_operand_aliasing={{0}: (0, {}), {1}: (1, {}), {2}: (2, {})} | custom-call | flops 4194304 | bytes 6291456 | tf_op jit(solution)/shard_map/pallas_call | solution.py:428
  27.9 0.0 collective-permute-done.5.refs_3_
  27.9 2.1 %collective-permute-done.4.refs_2_ = f32[72,128]{1,0:T(8,128)S(1)} collective-permute-done((f32[72,128]{1,0:T(8,128)S(1)}, f32[72,128]{1,0:T(8,128)S(1)}, u32[]{:S(2)}, u32[]{:S(2)}) %collective-permute-start.4) | collective-permute-done | bytes 36896 | tf_op jit(solution)/shard_map/ppermute | solution.py:355
  30.0 0.0 collective-permute-done.3.refs_1_
  30.0 4.0 %collective-permute-start.6 = (f32[72,128]{1,0:T(8,128)S(1)}, f32[72,128]{1,0:T(8,128)S(1)}, u32[]{:S(2)}, u32[]{:S(2)}) collective-permute-start(f32[72,128]{1,0:T(8,128)S(1)} %shard_map.192.refs_1_), channel_id=1, source_target_pairs={{0,7},{1,6},{2,5},{3,4},{4,3},{5,2},{6,1},{7,0},{8,15},{9,14},{10,... | collective-permute-start | bytes 110600 | tf_op jit(solution)/shard_map/ppermute | solution.py:361
  34.0 1.7 %collective-permute-done.6.refs_2_ = f32[72,128]{1,0:T(8,128)S(1)} collective-permute-done((f32[72,128]{1,0:T(8,128)S(1)}, f32[72,128]{1,0:T(8,128)S(1)}, u32[]{:S(2)}, u32[]{:S(2)}) %collective-permute-start.6) | collective-permute-done | bytes 36896 | tf_op jit(solution)/shard_map/ppermute | solution.py:361
  35.7 0.1 shard_map.193
  35.8 9.6 %all_to_all.10.refs_0_ = f32[8,1,128]{2,1,0:T(1,128)S(1)} all-to-all(f32[8,1,128]{2,1,0:T(1,128)S(1)} %get-tuple-element.47), channel_id=1, replica_groups=mesh['y'=4,'core'=2,'x'=4,'z'=8] {'core','y'}, dimensions={0} | all-to-all | bytes 8192 | tf_op jit(solution)/shard_map/all_to_all | solution.py:350
  45.4 1.9 %shard_map.194 = (f32[4,512,128]{2,1,0:T(8,128)}, f32[2,320,512]{2,1,0:T(8,128)}, f32[1280,128]{1,0:T(8,128)}, f32[4,512]{1,0:T(4,128)}, f32[2,512]{1,0:T(2,128)}, /*index=5*/f32[10,128]{1,0:T(8,128)}) custom-call(f32[8,1,128]{2,1,0:T(1,128)S(1)} %all_to_all.10.refs_0_, f32[40,128]{1,0:T(8,128)S(1)} %get-tuple-element.48.refs_1_, ...), custom_call_target="tpu_custom_call" | custom-call | flops 4194304 | bytes 3145728 | tf_op jit(solution)/shard_map/pallas_call | solution.py:446
  (5 shorter events, 0.0 us)
Async XLA Ops:
  0.6 9.3 %copy-start = (f32[4,512]{1,0:T(4,128)S(1)}, f32[4,512]{1,0:T(4,128)}, u32[]{:S(2)}) copy-start(f32[4,512]{1,0:T(4,128)} %ar.1) | copy-start | bytes 24580
  0.7 9.3 %copy-start.1 = (f32[1280]{0:T(1024)S(1)}, f32[1280]{0:T(1024)}, u32[]{:S(2)}) copy-start(f32[1280]{0:T(1024)} %param.22) | copy-start | bytes 15364
  0.7 9.3 %copy-start.2 = (f32[2,512]{1,0:T(2,128)S(1)}, f32[2,512]{1,0:T(2,128)}, u32[]{:S(2)}) copy-start(f32[2,512]{1,0:T(2,128)} %wr.1) | copy-start | bytes 12292
  0.7 9.3 %copy-start.3 = (f32[2,320]{1,0:T(2,128)S(1)}, f32[2,320]{1,0:T(2,128)}, u32[]{:S(2)}) copy-start(f32[2,320]{1,0:T(2,128)} %wc.1) | copy-start | bytes 7684
  0.7 9.3 %copy-start.4 = (f32[4,128]{1,0:T(4,128)S(1)}, f32[4,128]{1,0:T(4,128)}, u32[]{:S(2)}) copy-start(f32[4,128]{1,0:T(4,128)} %ac.1) | copy-start | bytes 6148
  0.7 9.3 %copy-start.5 = (f32[128]{0:T(128)S(1)}, f32[128]{0:T(128)}, u32[]{:S(2)}) copy-start(f32[128]{0:T(128)} %param.23) | copy-start | bytes 1540
  3.4 11.4 %all-to-all-start = ((f32[8,1,1408]{2,1,0:T(1,128)}), f32[8,1,1408]{2,1,0:T(1,128)S(1)}, u32[]{:S(2)}, u32[]{:S(2)}) async-start(f32[8,1,1408]{2,1,0:T(1,128)} %get-tuple-element.41), calls=%async_computation | async-start | bytes 90112 | tf_op jit(solution)/shard_map/all_to_all | solution.py:350
  15.3 5.3 %collective-permute-start.2 = (f32[72,128]{1,0:T(8,128)S(1)}, f32[72,128]{1,0:T(8,128)S(1)}, u32[]{:S(2)}, u32[]{:S(2)}) collective-permute-start(f32[72,128]{1,0:T(8,128)S(1)} %get-tuple-element.45.own), channel_id=1, source_target_pairs={{0,3},{1,2},{2,1},{3,0},{4,7},{5,6},{6,5},{7,4},{8,11},{9,10},{10,... | collective-permute-start | bytes 110600 | tf_op jit(solution)/shard_map/ppermute | solution.py:355
  19.2 3.9 %collective-permute-start.1 = (f32[72,128]{1,0:T(8,128)S(1)}, f32[72,128]{1,0:T(8,128)S(1)}, u32[]{:S(2)}, u32[]{:S(2)}) collective-permute-start(f32[72,128]{1,0:T(8,128)S(1)} %get-tuple-element.45.own), channel_id=1, source_target_pairs={{0,2},{1,3},{2,0},{3,1},{4,6},{5,7},{6,4},{7,5},{8,10},{9,11},{10,... | collective-permute-start | bytes 110600 | tf_op jit(solution)/shard_map/ppermute | solution.py:355
  19.2 3.9 %collective-permute-start = (f32[72,128]{1,0:T(8,128)S(1)}, f32[72,128]{1,0:T(8,128)S(1)}, u32[]{:S(2)}, u32[]{:S(2)}) collective-permute-start(f32[72,128]{1,0:T(8,128)S(1)} %get-tuple-element.45.own), channel_id=1, source_target_pairs={{0,1},{1,0},{2,3},{3,2},{4,5},{5,4},{6,7},{7,6},{8,9},{9,8},{10,11... | collective-permute-start | bytes 110600 | tf_op jit(solution)/shard_map/ppermute | solution.py:355
  23.1 4.8 %collective-permute-start.5 = (f32[72,128]{1,0:T(8,128)S(1)}, f32[72,128]{1,0:T(8,128)S(1)}, u32[]{:S(2)}, u32[]{:S(2)}) collective-permute-start(f32[72,128]{1,0:T(8,128)S(1)} %shard_map.190.after.refs_0_), channel_id=1, source_target_pairs={{0,16},{8,24},{16,0},{24,8},{1,17},{9,25},{17,1},{25,9},{2,18},{10... | collective-permute-start | bytes 110600 | tf_op jit(solution)/shard_map/ppermute | solution.py:355
  25.9 4.0 %collective-permute-start.4 = (f32[72,128]{1,0:T(8,128)S(1)}, f32[72,128]{1,0:T(8,128)S(1)}, u32[]{:S(2)}, u32[]{:S(2)}) collective-permute-start(f32[72,128]{1,0:T(8,128)S(1)} %shard_map.190.after.refs_0_), channel_id=1, source_target_pairs={{0,24},{8,16},{16,8},{24,0},{1,25},{9,17},{17,9},{25,1},{2,26},{10... | collective-permute-start | bytes 110600 | tf_op jit(solution)/shard_map/ppermute | solution.py:355
  26.8 3.2 %collective-permute-start.3 = (f32[72,128]{1,0:T(8,128)S(1)}, f32[72,128]{1,0:T(8,128)S(1)}, u32[]{:S(2)}, u32[]{:S(2)}) collective-permute-start(f32[72,128]{1,0:T(8,128)S(1)} %shard_map.190.after.refs_0_), channel_id=1, source_target_pairs={{0,8},{8,0},{16,24},{24,16},{1,9},{9,1},{17,25},{25,17},{2,10},{10... | collective-permute-start | bytes 110600 | tf_op jit(solution)/shard_map/ppermute | solution.py:355
  30.0 5.7 %collective-permute-start.6 = (f32[72,128]{1,0:T(8,128)S(1)}, f32[72,128]{1,0:T(8,128)S(1)}, u32[]{:S(2)}, u32[]{:S(2)}) collective-permute-start(f32[72,128]{1,0:T(8,128)S(1)} %shard_map.192.refs_1_), channel_id=1, source_target_pairs={{0,7},{1,6},{2,5},{3,4},{4,3},{5,2},{6,1},{7,0},{8,15},{9,14},{10,... | collective-permute-start | bytes 110600 | tf_op jit(solution)/shard_map/ppermute | solution.py:361
